TPU v7x, 512 devices: a whole 4x4x16 slice. The times are simulated.
512 devices in a mesh: replica: 8 (over x, core), shard: 16 (over z), tensor: 4 (over y).
Axes of the slice: x: 4, y: 4, z: 16, core: 2. Of those that a mesh axis runs over, the one named last changes fastest.
Arguments:
- gradients: bfloat16 [8, 64, 512, 512], P('replica', None, ('shard', 'tensor')), may hold values from -2 to 2
- old_stats: float32 [128, 2, 512, 512], P(('shard', 'tensor'), None, 'replica'), as said below
- owner_slot: int32 [64], replicated, may hold values from 0 to 127, as said below
Outputs:
- updates: bfloat16 [64, 512, 512], P(None, ('shard', 'tensor'))
Inputs may be any that keep to these rules, and one draw needn't show every extreme that they name: `old_stats`: symmetric positive definite in every slot and side. `owner_slot`: values are distinct; some owner holds 2 blocks.
All inputs are finite; a program needn't handle non-finite values.
Results may differ from a plain program's by a relative error of at most 0.02.
Values may be sent and summed in bfloat16 or wider, within the bound.
No kernel may reach another device: no remote copies, remote signals or barrier semaphores. Data moves between devices by JAX's collectives and lax.ppermute only.
A program may use at most 64 MiB of HBM per device.

v0:
```python
import jax
import jax.numpy as jnp
from jax import lax
from jax.sharding import PartitionSpec as P

NEWTON = 2


ridge_term = 1e-06
decay_rate = 0.95
graft_floor = 1e-06
start_scale = 4.0


def product(left, right):
    return jnp.einsum("nij,njk->nik", left, right, preferred_element_type=jnp.float32)


def inverse_root(matrices):
    block_order = matrices.shape[-1]
    identity = jnp.eye(block_order, dtype=jnp.float32)
    shifted = matrices + ridge_term * identity
    norm_size = jnp.sqrt(jnp.sum(shifted * shifted, axis=(1, 2), keepdims=True))
    iterate = start_scale * shifted / norm_size
    root_now = None
    for newton_step in range(NEWTON):
        factor = ((5.0 * identity - iterate) / 4.0).astype(jnp.bfloat16)
        if newton_step == 0:
            root_now = factor
        else:
            root_now = product(root_now, factor).astype(jnp.bfloat16)
        if newton_step + 1 < NEWTON:
            square = product(factor, factor).astype(jnp.bfloat16)
            fourth = product(square, square).astype(jnp.bfloat16)
            iterate = product(fourth, iterate.astype(jnp.bfloat16))
    return root_now


def on_device(gradients, old_stats, owner_slot):
    shard_grads = gradients[0]
    block_count, local_rows, block_order = shard_grads.shape
    slot_count = old_stats.shape[0]
    replica_rows = old_stats.shape[2]
    owner_count = lax.axis_size(("shard", "tensor"))
    total_slots = owner_count * slot_count
    slot_ids = jnp.arange(total_slots, dtype=jnp.int32)
    matches = owner_slot[None, :] == slot_ids[:, None]
    present = jnp.any(matches, axis=1)[:, None, None]
    sources = jnp.sum(
        jnp.where(matches, jnp.arange(block_count, dtype=jnp.int32)[None, :], 0), axis=1
    )
    summed = lax.psum(shard_grads.astype(jnp.float32).astype(jnp.bfloat16), "replica").astype(
        jnp.float32
    )
    outgoing = jnp.where(present, summed[sources], 0.0).reshape(
        owner_count, slot_count, local_rows, block_order
    )
    grad_sum = (
        lax.all_to_all(
            outgoing.astype(jnp.bfloat16),
            ("shard", "tensor"),
            split_axis=0,
            concat_axis=2,
            tiled=True,
        )
        .astype(outgoing.dtype)
        .reshape(slot_count, block_order, block_order)
    )
    grad_low = grad_sum.astype(jnp.bfloat16)
    replica_index = lax.axis_index("replica")
    row_block = lax.dynamic_slice_in_dim(grad_low, replica_index * replica_rows, replica_rows, 1)
    column_block = lax.dynamic_slice_in_dim(grad_low, replica_index * replica_rows, replica_rows, 2)
    left_rows = decay_rate * old_stats[:, 0] + jnp.einsum(
        "srk,sjk->srj", row_block, grad_low, preferred_element_type=jnp.float32
    )
    right_rows = decay_rate * old_stats[:, 1] + jnp.einsum(
        "sko,skj->soj", column_block, grad_low, preferred_element_type=jnp.float32
    )
    stacked = jnp.stack([left_rows, right_rows], axis=1).reshape(
        2 * slot_count, replica_rows, block_order
    )
    root_pairs = inverse_root(lax.all_gather(stacked, "replica", axis=1, tiled=True))
    root_pairs = root_pairs.reshape(slot_count, 2, block_order, block_order)
    half_product = jnp.einsum(
        "sij,sjk->sik", root_pairs[:, 0], grad_low, preferred_element_type=jnp.float32
    ).astype(jnp.bfloat16)
    precond = jnp.einsum(
        "sij,sjk->sik", half_product, root_pairs[:, 1], preferred_element_type=jnp.float32
    )
    mean_grad = jnp.mean(grad_sum * grad_sum, axis=(1, 2), keepdims=True)
    mean_pre = jnp.mean(precond * precond, axis=(1, 2), keepdims=True)
    updates = (precond * jnp.sqrt(mean_grad) / jnp.sqrt(mean_pre + graft_floor)).astype(
        jnp.bfloat16
    )
    outgoing_back = updates.reshape(slot_count, owner_count, local_rows, block_order)
    returned = lax.all_to_all(
        outgoing_back, ("shard", "tensor"), split_axis=1, concat_axis=0, tiled=True
    )
    return returned.reshape(total_slots, local_rows, block_order)[owner_slot]


def solution(mesh):
    placed = (
        P("replica", None, ("shard", "tensor"), None),
        P(("shard", "tensor"), None, "replica", None),
        P(),
    )
    return jax.shard_map(
        on_device,
        mesh=mesh,
        in_specs=placed,
        out_specs=P(None, ("shard", "tensor"), None),
        check_vma=False,
    )
```

profile of v0, /device:TPU:1, one launch (start us, length us, event | category | flops | bytes accessed | tf_op | source)
XLA Modules:
  0.0 302.7 jit_solution(4919680536329502781)
XLA Ops:
  6.5 0.0 all-reduce.2.cloned.1.call-start
  6.5 0.7 all-reduce.2.cloned.1.call-update
  7.3 0.7 select_reduce_fusion
  8.0 0.7 fusion.20
  8.7 0.2 broadcast_in_dim.40
  8.9 0.0 copy-start
  8.9 80.6 %all-reduce.2.cloned.1.call-done = bf16[64,8,512]{2,1,0:T(8,128)(2,1)} async-done(((bf16[64,8,512]{2,1,0:T(8,128)(2,1)}), bf16[64,8,512]{2,1,0:T(8,128)(2,1)}) %all-reduce.2.cloned.1.call-update) | async-done | bytes 524304 | tf_op jit(solution)/shard_map/psum | solution.py:52
  89.6 1.7 gather_fusion
  91.3 1.3 select_convert_fusion
  92.6 14.8 %all-to-all-start = ((bf16[64,2,8,512]{3,2,1,0:T(8,128)(2,1)}), bf16[64,2,8,512]{3,2,1,0:T(8,128)(2,1)S(1)}, u32[]{:S(2)}, u32[]{:S(2)}) async-start(bf16[64,2,8,512]{3,2,1,0:T(8,128)(2,1)} %select_convert_fusion), calls=%async_computation | async-start | bytes 2097152 | tf_op jit(solution)/shard_map/all_to_all | solution.py:59
  107.4 0.0 all-gather.2.cloned.1.call-start
  107.5 49.2 %all-to-all-done = bf16[64,2,8,512]{3,2,1,0:T(8,128)(2,1)S(1)} async-done(((bf16[64,2,8,512]{3,2,1,0:T(8,128)(2,1)}), bf16[64,2,8,512]{3,2,1,0:T(8,128)(2,1)S(1)}, u32[]{:S(2)}, u32[]{:S(2)}) %all-to-all-start) | async-done | bytes 1048608 | tf_op jit(solution)/shard_map/all_to_all | solution.py:59
  156.7 0.1 copy_bitcast_fusion
  156.7 0.0 copy-done
  156.8 0.4 fusion.7
  157.2 0.4 fusion.8
  157.7 0.8 copy.30
  158.5 0.0 all-gather.2.cloned.1.call-update
  158.5 0.2 fusion.9
  158.8 0.4 multiply_reduce_fusion.2
  159.2 38.0 %all-gather.2.cloned.1.call-done = f32[4,512,512]{2,1,0:T(8,128)} async-done(((f32[4,64,512]{2,1,0:T(8,128)}), f32[4,512,512]{2,1,0:T(8,128)}) %all-gather.2.cloned.1.call-update) | async-done | bytes 4194320 | tf_op jit(solution)/shard_map/all_gather | solution.py:82
  197.2 3.0 %multiply_reduce_fusion = f32[4]{0:T(128)S(1)} fusion(f32[4,512,512]{2,1,0:T(8,128)} %all-gather.2.cloned.1.call-done, f32[512,512]{1,0:T(8,128)S(1)} %get-tuple-element.7), kind=kLoop, calls=%fused_computation.4 | loop fusion | flops 3145724 | bytes 5242896 | tf_op jit(solution)/shard_map/reduce_sum | solution.py:23
  200.3 13.1 %fusion.2 = bf16[4,512,512]{2,1,0:T(8,128)(2,1)} fusion(f32[512,512]{1,0:T(8,128)S(1)} %get-tuple-element.8, f32[4,512,512]{2,1,0:T(8,128)} %all-gather.2.cloned.1.call-done, f32[4]{0:T(128)S(1)} %sqrt.24, f32[512,512]{1,0:T(8,128)S(1)} %get-tuple-element.7), kind=kOutput, calls=%fused_computation.11 | convolution fusion | flops 2154823680 | bytes 8388624 | tf_op jit(solution)/shard_map/nij,njk->nik/dot_general | solution.py:16
  213.4 8.6 %convolution_convert_fusion = bf16[4,512,512]{2,1,0:T(8,128)(2,1)} fusion(bf16[4,512,512]{2,1,0:T(8,128)(2,1)} %fusion.2, f32[512,512]{1,0:T(8,128)S(1)} %get-tuple-element.8, f32[4,512,512]{2,1,0:T(8,128)} %all-gather.2.cloned.1.call-done, f32[4]{0:T(128)S(1)} %sqrt.24, f32[512,512]{1,0:T(8,128)S(1)} %get-tuple-element.7), kind=kOutput, calls=%fused_computation.14 | convolution fusion | flops 2162163712 | bytes 10485776 | tf_op jit(solution)/shard_map/nij,njk->nik/dot_general | solution.py:16
  222.0 3.0 multiply_reduce_fusion.1
  225.0 0.0 copy-start.1
  225.0 0.4 fusion.11
  225.4 1.1 copy.33
  226.5 15.4 %all-to-all-start.1 = ((bf16[2,64,8,512]{3,2,0,1:T(8,128)(2,1)}), bf16[2,64,8,512]{3,2,0,1:T(8,128)(2,1)S(1)}, u32[]{:S(2)}, u32[]{:S(2)}) async-start(bf16[2,64,8,512]{3,2,0,1:T(8,128)(2,1)} %copy.33), calls=%async_computation.1 | async-start | bytes 2097152 | tf_op jit(solution)/shard_map/all_to_all | solution.py:96
  241.9 0.0 copy-done.1
  241.9 52.6 %all-to-all-done.1 = bf16[2,64,8,512]{3,2,0,1:T(8,128)(2,1)S(1)} async-done(((bf16[2,64,8,512]{3,2,0,1:T(8,128)(2,1)}), bf16[2,64,8,512]{3,2,0,1:T(8,128)(2,1)S(1)}, u32[]{:S(2)}, u32[]{:S(2)}) %all-to-all-start.1) | async-done | bytes 1048608 | tf_op jit(solution)/shard_map/all_to_all | solution.py:96
  294.5 1.4 gather_fusion.1
  (8 shorter events, 0.1 us)
Async XLA Ops:
  6.5 83.0 %all-reduce.2.cloned.1.call-start = ((), (), s32[]{:S(2)}) async-start(), calls=%async_computation.2 | async-start | bytes 1048576 | tf_op jit(solution)/shard_map/psum | solution.py:52
  8.9 147.8 %copy-start = (f32[2,2,64,512]{3,2,1,0:T(8,128)S(1)}, f32[2,2,64,512]{3,2,1,0:T(8,128)}, u32[]{:S(2)}) copy-start(f32[2,2,64,512]{3,2,1,0:T(8,128)} %param.4) | copy-start | bytes 1572868
  92.6 64.1 %all-to-all-start = ((bf16[64,2,8,512]{3,2,1,0:T(8,128)(2,1)}), bf16[64,2,8,512]{3,2,1,0:T(8,128)(2,1)S(1)}, u32[]{:S(2)}, u32[]{:S(2)}) async-start(bf16[64,2,8,512]{3,2,1,0:T(8,128)(2,1)} %select_convert_fusion), calls=%async_computation | async-start | bytes 2097152 | tf_op jit(solution)/shard_map/all_to_all | solution.py:59
  107.4 89.8 %all-gather.2.cloned.1.call-start = ((), (), s32[]{:S(2)}) async-start(), calls=%async_computation.3 | async-start | bytes 4718592 | tf_op jit(solution)/shard_map/all_gather | solution.py:82
  225.0 16.9 %copy-start.1 = (s32[64]{0:T(128)S(1)}, s32[64]{0:T(128)}, u32[]{:S(2)}) copy-start(s32[64]{0:T(128)} %param.5) | copy-start | bytes 772
  226.5 68.0 %all-to-all-start.1 = ((bf16[2,64,8,512]{3,2,0,1:T(8,128)(2,1)}), bf16[2,64,8,512]{3,2,0,1:T(8,128)(2,1)S(1)}, u32[]{:S(2)}, u32[]{:S(2)}) async-start(bf16[2,64,8,512]{3,2,0,1:T(8,128)(2,1)} %copy.33), calls=%async_computation.1 | async-start | bytes 2097152 | tf_op jit(solution)/shard_map/all_to_all | solution.py:96
Sparse Core Ops, SparseCore 0:
  9.7 79.8 all-reduce.1
  158.7 38.5 all-gather.1
where the time goes:
time: 305 us; the launch traced here: 303 us
  waiting for transfers between devices  221 us (72%)
  starting transfers between devices  30.2 us (10%)
  matrix products  25.6 us (8%)
  between operations  13.5 us (4%)
  other arithmetic  6.93 us (2%)
  local copies, waits for them, and re-layouts  5.27 us (2%)
    psum x1, waiting for transfers between devices, on_device(): lax.psum(shard_grads.astype(jnp.float32).astype(jnp.bfloat16), 'replica')  80.6 us
    all_to_all x1, waiting for transfers between devices, on_device(): lax.all_to_all(outgoing_back, ('shard', 'tensor'), split_axis=1, concat_a...  52.6 us
    all_to_all x1, waiting for transfers between devices, on_device(): lax.all_to_all(outgoing.astype(jnp.bfloat16), ('shard', 'tensor'), split_...  49.2 us
    all_gather x1, waiting for transfers between devices, on_device(): lax.all_gather(stacked, 'replica', axis=1, tiled=True)  38 us
    dot_general x2, matrix products, product(): jnp.einsum('nij,njk->nik', left, right, preferred_element_type=jnp.float32)  21.7 us
    all_to_all x1, starting transfers between devices, on_device(): lax.all_to_all(outgoing_back, ('shard', 'tensor'), split_axis=1, concat_a...  15.4 us
    all_to_all x1, starting transfers between devices, on_device(): lax.all_to_all(outgoing.astype(jnp.bfloat16), ('shard', 'tensor'), split_...  14.8 us
  transfers between devices with their start and end apart: 4, of which 4 were waited for; matrix products, arithmetic and copies ran while one was open for 1% of the time, Pallas kernels for 0%

commit v1 on v0

v1 whole, which is shorter than its diff:
```python
import jax
import jax.numpy as jnp
from jax import lax
from jax.experimental import pallas as pl
from jax.experimental.pallas import tpu as pltpu
from jax.sharding import Mesh, PartitionSpec as P

ridge_term = 1e-06
decay_rate = 0.95
graft_floor = 1e-06
start_scale = 4.0

BF = jnp.bfloat16
F32 = jnp.float32
VMEM_LIMIT = 48 * 1024 * 1024


def call(kernel, out_shape, in_kinds, scratch=(), flops=0, nbytes=1 << 20):
    kinds = {"v": pltpu.VMEM, "s": pltpu.SMEM}
    single = not isinstance(out_shape, (list, tuple))
    spec = pl.BlockSpec(memory_space=pltpu.VMEM)
    return pl.pallas_call(
        kernel,
        out_shape=out_shape,
        in_specs=[pl.BlockSpec(memory_space=kinds[k]) for k in in_kinds],
        out_specs=spec if single else [spec] * len(out_shape),
        scratch_shapes=list(scratch),
        compiler_params=pltpu.CompilerParams(vmem_limit_bytes=VMEM_LIMIT),
        cost_estimate=pl.CostEstimate(flops=flops, bytes_accessed=nbytes, transcendentals=0),
    )


def place_kernel(ny, nz, slot_ref, core_ref, grad_ref, stat_ref, keep_ref, send_ref):
    blocks = grad_ref.shape[0]
    owners = ny * nz
    core = core_ref[0]
    keep_ref[:owners] = jnp.zeros((owners,) + keep_ref.shape[1:], BF)
    send_ref[:owners] = jnp.zeros((owners,) + keep_ref.shape[1:], BF)

    def step(block, carry):
        slot = slot_ref[block]
        owner = slot // 2
        place = (owner % ny) * nz + owner // ny
        mine = slot % 2 == core

        @pl.when(mine)
        def _():
            keep_ref[place] = grad_ref[block]

        @pl.when(jnp.logical_not(mine))
        def _():
            send_ref[place] = grad_ref[block]

        return carry

    lax.fori_loop(0, blocks, step, 0, unroll=4)
    tail = keep_ref.shape[0] - owners
    tail_shape = (tail,) + keep_ref.shape[1:]
    keep_ref[owners:] = stat_ref[core].reshape(tail_shape).astype(BF)
    send_ref[owners:] = stat_ref[1 - core].reshape(tail_shape).astype(BF)


def quarter_kernel(nx, core_ref, keep_ref, got_ref, out_ref, stat_ref):
    owners = out_ref.shape[1] * out_ref.shape[2]
    width = out_ref.shape[-1]
    core = core_ref[0]
    for part in range(nx):
        cols = slice(part * width, (part + 1) * width)
        total = keep_ref[:owners, :, cols].astype(F32) + got_ref[:owners, :, cols].astype(F32)
        out_ref[part] = total.astype(BF).reshape(out_ref.shape[1:])
    stat_ref[core] = keep_ref[owners:]
    stat_ref[1 - core] = got_ref[owners:]


def sum_kernel(in_ref, out_ref):
    nx, ny = in_ref.shape[:2]
    for part in range(ny):
        total = in_ref[0, part].astype(F32)
        for copy in range(1, nx):
            total = total + in_ref[copy, part].astype(F32)
        out_ref[:, part] = total.astype(BF)


def dot(left, right, contract=((1,), (0,))):
    return lax.dot_general(left, right, (contract, ((), ())), preferred_element_type=F32)


def step_kernel(nx, place_ref, quarter_ref, *refs):
    stat_refs, (out_ref, grad_ref, stats) = refs[:nx], refs[nx:]
    order = grad_ref.shape[0]
    width = quarter_ref.shape[-1]
    rows = order // nx
    x = place_ref[1]
    for part in range(nx):
        grad_ref[:, part * width : (part + 1) * width] = quarter_ref[part]
    for shift in range(nx):
        source = lax.rem(x - shift + nx, nx)
        for core in range(2):
            start = pl.multiple_of(source * rows + core * (rows // 2), rows // 2)
            for side in range(2):
                stats[side, pl.ds(start, rows // 2), :] = stat_refs[shift][core, side]
    grad = grad_ref[...]
    row_ids = lax.broadcasted_iota(jnp.int32, (order, order), 0)
    col_ids = lax.broadcasted_iota(jnp.int32, (order, order), 1)
    diagonal = row_ids == col_ids
    roots = []
    for side in range(2):
        gram = dot(grad, grad, ((1,), (1,)) if side == 0 else ((0,), (0,)))
        shifted = decay_rate * stats[side].astype(F32) + gram + jnp.where(diagonal, ridge_term, 0.0)
        scale = start_scale * lax.rsqrt(jnp.sum(shifted * shifted))
        iterate = shifted * scale
        factor = (jnp.where(diagonal, 1.25, 0.0) - 0.25 * iterate).astype(BF)
        square = dot(factor, factor).astype(BF)
        fourth = dot(square, square).astype(BF)
        iterate = dot(fourth, iterate.astype(BF))
        second = (jnp.where(diagonal, 1.25, 0.0) - 0.25 * iterate).astype(BF)
        roots.append(dot(factor, second).astype(BF))
    half = dot(roots[0], grad).astype(BF)
    precond = dot(half, roots[1])
    count = float(order * order)
    grad32 = grad.astype(F32)
    mean_grad = jnp.sum(grad32 * grad32) / count
    mean_pre = jnp.sum(precond * precond) / count
    scale = jnp.sqrt(mean_grad) / jnp.sqrt(mean_pre + graft_floor)
    for part in range(nx):

        @pl.when(x == part)
        def _():
            out_ref[...] = (precond[:, part * width : (part + 1) * width] * scale).astype(BF)


def spread_kernel(in_ref, out_ref):
    nx, ny = out_ref.shape[:2]
    for part in range(ny):
        piece = in_ref[:, part]
        for copy in range(nx):
            out_ref[copy, part] = piece


def pick_kernel(ny, slot_ref, core_ref, own_ref, got_ref, out_ref):
    nx = own_ref.shape[0]
    width = own_ref.shape[-1]
    core = core_ref[0]

    def step(block, carry):
        slot = slot_ref[block]
        owner = slot // 2
        y, z = owner % ny, owner // ny
        mine = slot % 2 == core

        @pl.when(mine)
        def _():
            for part in range(nx):
                out_ref[block, :, part * width : (part + 1) * width] = own_ref[part, y, z]

        @pl.when(jnp.logical_not(mine))
        def _():
            for part in range(nx):
                out_ref[block, :, part * width : (part + 1) * width] = got_ref[part, y, z]

        return carry

    lax.fori_loop(0, out_ref.shape[0], step, 0, unroll=4)


def shaped(shape, dtype=BF):
    return jax.ShapeDtypeStruct(shape, dtype)


def on_device(gradients, old_stats, owner_slot):
    nx, nz, ny = lax.axis_size("x"), lax.axis_size("shard"), lax.axis_size("tensor")
    grads = gradients[0]
    blocks, rows, order = grads.shape
    owners = ny * nz
    width = order // nx
    stat_rows = old_stats.shape[2]
    tail = 2 * stat_rows // rows
    here = jnp.stack([lax.axis_index("core"), lax.axis_index("x")]).astype(jnp.int32)
    swap = [(0, 1), (1, 0)]

    def place(*refs):
        place_kernel(ny, nz, *refs)

    whole = (owners + tail, rows, order)
    keep, send = call(place, [shaped(whole), shaped(whole)], "ssvv")(owner_slot, here, grads, old_stats)
    got = lax.ppermute(send, "core", swap)

    def quarter(*refs):
        quarter_kernel(nx, *refs)

    parts, stat = call(
        quarter, [shaped((nx, ny, nz, rows, width)), shaped((2, tail, rows, order))], "svv"
    )(here, keep, got)
    parts = lax.all_to_all(
        parts.reshape(nx * ny, nz, rows, width), ("x", "tensor"), split_axis=0, concat_axis=0, tiled=True
    ).reshape(nx, ny, nz, rows, width)
    stat = stat.reshape(2, 2, stat_rows, order)
    stats = [stat] + [
        lax.ppermute(stat, "x", [(i, (i + shift) % nx) for i in range(nx)]) for shift in range(1, nx)
    ]
    summed = call(sum_kernel, shaped((nz, ny, rows, width)), "v")(parts)
    quarter_grad = lax.all_to_all(summed, "shard", split_axis=0, concat_axis=0, tiled=True)
    quarter_grad = quarter_grad.reshape(1, order, width)
    quarters = lax.all_to_all(
        jnp.broadcast_to(quarter_grad, (nx, order, width)), "x", split_axis=0, concat_axis=0, tiled=True
    )

    def step(*refs):
        step_kernel(nx, *refs)

    update = call(
        step,
        shaped((order, width)),
        "sv" + "v" * nx,
        scratch=[pltpu.VMEM((order, order), BF), pltpu.VMEM((2, order, order), BF)],
        flops=24 * order**3,
        nbytes=2 << 20,
    )(here, quarters, *stats)
    back = lax.all_to_all(
        update.reshape(nz, ny, rows, width), "shard", split_axis=0, concat_axis=0, tiled=True
    )
    spread = call(spread_kernel, shaped((nx, ny, nz, rows, width)), "v")(back)
    own = lax.all_to_all(
        spread.reshape(nx * ny, nz, rows, width), ("x", "tensor"), split_axis=0, concat_axis=0, tiled=True
    ).reshape(nx, ny, nz, rows, width)
    other = lax.ppermute(own, "core", swap)

    def pick(*refs):
        pick_kernel(ny, *refs)

    return call(pick, shaped((blocks, rows, order)), "ssvv")(owner_slot, here, own, other)


def solution(mesh):
    replica, nz, ny = (mesh.shape[name] for name in ("replica", "shard", "tensor"))
    fine = Mesh(mesh.devices.reshape(replica // 2, 2, nz, ny), ("x", "core", "shard", "tensor"))
    replicas, rows = ("x", "core"), ("shard", "tensor")
    return jax.shard_map(
        on_device,
        mesh=fine,
        in_specs=(P(replicas, None, rows, None), P(rows, None, replicas, None), P()),
        out_specs=P(None, rows, None),
        check_vma=False,
    )
```

time: 305 us -> 126 us (0.41)
  waiting for transfers between devices: 221 us -> 10.7 us
  blocking collectives: 0 us -> 69.4 us
  matrix products: 25.6 us -> 0 us
  between operations: 13.5 us -> 0.08 us
  Pallas kernels: 0 us -> 12 us
  other arithmetic: 6.93 us -> 0.07 us
    all_to_all x2 -> x1, waiting for transfers between devices: 102 us -> 0.01 us  [on_device(): lax.all_to_all(jnp.broadcast_to(quarter_grad, (nx, order, width)), 'x', s...]
    psum x1 -> x0, waiting for transfers between devices: 80.6 us -> none  [on_device(): lax.psum(shard_grads.astype(jnp.float32).astype(jnp.bfloat16), 'replica')]
    all_to_all x0 -> x4, blocking collectives: none -> 69.4 us  [the longest x1 25.4 us: on_device(): lax.all_to_all(summed, 'shard', split_axis=0, concat_axis=0, tiled=True)]
    all_gather x1 -> x0, waiting for transfers between devices: 38 us -> none  [on_device(): lax.all_gather(stacked, 'replica', axis=1, tiled=True)]
    all_to_all x2 -> x1, starting transfers between devices: 30.2 us -> 3.47 us  [on_device(): lax.all_to_all(jnp.broadcast_to(quarter_grad, (nx, order, width)), 'x', s...]
    ppermute x0 -> x5, starting transfers between devices: none -> 26.4 us  [the longest x3 10.7 us: on_device(): lax.ppermute(stat, 'x', [(i, (i + shift) % nx) for i in range(nx)])]
    dot_general x5 -> x0, matrix products: 25.6 us -> none  [the longest x2 21.7 us: product(): jnp.einsum('nij,njk->nik', left, right, preferred_element_type=jnp.float32)]
    pallas_call x0 -> x6, Pallas kernels: none -> 12 us  [the longest x1 5.86 us: on_device(): call(step, shaped((order, width)), 'sv' + 'v' * nx, scratch=[pltpu.VMEM((...]
  transfers between devices with their start and end apart: 4 -> 6, of which waited for: 4 -> 5; matrix products, arithmetic and copies ran while one was open for 1% -> 0% of each run, Pallas kernels for 0% -> 0%
where the time goes in v1:
time: 126 us
  blocking collectives  69.4 us (55%)
  starting transfers between devices  29.9 us (24%)
  Pallas kernels  12 us (10%)
  waiting for transfers between devices  10.7 us (8%)
  local copies, waits for them, and re-layouts  3.6 us (3%)
    all_to_all x1, blocking collectives, on_device(): lax.all_to_all(summed, 'shard', split_axis=0, concat_axis=0, tiled=True)  25.4 us
    all_to_all x1, blocking collectives, on_device(): lax.all_to_all(spread.reshape(nx * ny, nz, rows, width), ('x', 'tensor'),...  15.7 us
    all_to_all x1, blocking collectives, on_device(): lax.all_to_all(update.reshape(nz, ny, rows, width), 'shard', split_axis=0...  15.4 us
    all_to_all x1, blocking collectives, on_device(): lax.all_to_all(parts.reshape(nx * ny, nz, rows, width), ('x', 'tensor'),...  12.9 us
    ppermute x3, starting transfers between devices, on_device(): lax.ppermute(stat, 'x', [(i, (i + shift) % nx) for i in range(nx)])  10.7 us
    ppermute x1, starting transfers between devices, on_device(): got = lax.ppermute(send, 'core', swap)  8.78 us
    ppermute x3, waiting for transfers between devices, on_device(): lax.ppermute(stat, 'x', [(i, (i + shift) % nx) for i in range(nx)])  7.51 us
    ppermute x1, starting transfers between devices, on_device(): other = lax.ppermute(own, 'core', swap)  6.95 us
  transfers between devices with their start and end apart: 6, of which 5 were waited for; matrix products, arithmetic and copies ran while one was open for 0% of the time, Pallas kernels for 0%

profile of v1, /device:TPU:1, one launch (start us, length us, event | category | flops | bytes accessed | tf_op | source)
XLA Modules:
  0.0 125.7 jit_solution(1816005945166506822)
XLA Ops:
  0.0 0.1 pad_add_fusion.refs_1_.refs_0_
  0.1 0.0 copy-start.2
  0.1 0.7 copy-done.2
  0.7 0.0 copy-start
  0.7 1.0 copy-done
  1.8 0.0 copy-start.1
  1.8 1.0 copy-done.1
  2.8 2.2 %shard_map.37 = (bf16[80,8,512]{2,1,0:T(8,128)(2,1)S(1)}, bf16[80,8,512]{2,1,0:T(8,128)(2,1)S(1)}) custom-call(s32[64]{0:T(128)S(1)} %copy-done.2, s32[2]{0:T(128)S(1)} %pad_add_fusion.refs_1_.refs_0_, bf16[64,8,512]{2,1,0:T(8,128)(2,1)S(1)} %bitcast.14, f32[2,2,64,512]{3,2,1,0:T(8,128)S(1)} %copy-done.1), custom_call_target="tpu_custom_call" | custom-call | bytes 1048576 | tf_op jit(solution)/shard_map/pallas_call | solution.py:185
  5.1 8.8 %collective-permute-start = (bf16[80,8,512]{2,1,0:T(8,128)(2,1)S(1)}, bf16[80,8,512]{2,1,0:T(8,128)(2,1)S(1)}, u32[]{:S(2)}, u32[]{:S(2)}) collective-permute-start(bf16[80,8,512]{2,1,0:T(8,128)(2,1)S(1)} %get-tuple-element.10), channel_id=1, source_target_pairs={{0,64},{64,0},{1,65},{65,1},{2,66},{66,2},{3,67},{67,3},{4,68},{68... | collective-permute-start | bytes 1966088 | tf_op jit(solution)/shard_map/ppermute | solution.py:186
  13.8 1.7 %collective-permute-done.refs_2_ = bf16[80,8,512]{2,1,0:T(8,128)(2,1)S(1)} collective-permute-done((bf16[80,8,512]{2,1,0:T(8,128)(2,1)S(1)}, bf16[80,8,512]{2,1,0:T(8,128)(2,1)S(1)}, u32[]{:S(2)}, u32[]{:S(2)}) %collective-permute-start) | collective-permute-done | bytes 655392 | tf_op jit(solution)/shard_map/ppermute | solution.py:186
  15.6 0.7 shard_map.38
  16.2 12.9 %all_to_all.25 = bf16[16,16,8,128]{3,2,1,0:T(8,128)(2,1)S(1)} all-to-all(bf16[16,16,8,128]{3,2,1,0:T(8,128)(2,1)S(1)} %bitcast.15), channel_id=1, replica_groups=mesh['x'=4,'core'=2,'shard'=16,'tensor'=4] {'x','tensor'}, dimensions={0} | all-to-all | bytes 1048576 | tf_op jit(solution)/shard_map/all_to_all | solution.py:194
  29.1 0.1 shard_map.39
  29.2 25.4 %all_to_all.26 = bf16[16,4,8,128]{3,2,1,0:T(8,128)(2,1)S(1)} all-to-all(bf16[16,4,8,128]{3,2,1,0:T(8,128)(2,1)S(1)} %shard_map.39), channel_id=1, replica_groups=mesh['x'=4,'core'=2,'shard'=16,'tensor'=4] {'shard'}, dimensions={0} | all-to-all | bytes 262144 | tf_op jit(solution)/shard_map/all_to_all | solution.py:202
  54.6 0.9 broadcast_in_dim.8
  55.4 3.5 %all-to-all-start.2 = ((bf16[4,512,128]{2,1,0:T(8,128)(2,1)}), bf16[4,512,128]{2,1,0:T(8,128)(2,1)S(1)}, u32[]{:S(2)}, u32[]{:S(2)}) async-start(bf16[4,512,128]{2,1,0:T(8,128)(2,1)} %broadcast_in_dim.8), calls=%async_computation.2 | async-start | bytes 1048576 | tf_op jit(solution)/shard_map/all_to_all | solution.py:204
  58.9 3.3 %collective-permute-start.1 = (bf16[2,2,64,512]{3,2,1,0:T(8,128)(2,1)S(1)}, bf16[2,2,64,512]{3,2,1,0:T(8,128)(2,1)S(1)}, u32[]{:S(2)}, u32[]{:S(2)}) collective-permute-start(bf16[2,2,64,512]{3,2,1,0:T(8,128)(2,1)S(1)} %bitcast.17), channel_id=1, source_target_pairs={{0,128},{128,256},{256,384},{384,0},{1,129},{129,257},{257,385},{3... | collective-permute-start | bytes 786440 | tf_op jit(solution)/shard_map/ppermute | solution.py:199
  62.2 4.3 %collective-permute-start.2 = (bf16[2,2,64,512]{3,2,1,0:T(8,128)(2,1)S(1)}, bf16[2,2,64,512]{3,2,1,0:T(8,128)(2,1)S(1)}, u32[]{:S(2)}, u32[]{:S(2)}) collective-permute-start(bf16[2,2,64,512]{3,2,1,0:T(8,128)(2,1)S(1)} %bitcast.18), channel_id=1, source_target_pairs={{0,256},{128,384},{256,0},{384,128},{1,257},{129,385},{257,1},{385... | collective-permute-start | bytes 786440 | tf_op jit(solution)/shard_map/ppermute | solution.py:199
  66.5 3.1 %collective-permute-start.3 = (bf16[2,2,64,512]{3,2,1,0:T(8,128)(2,1)S(1)}, bf16[2,2,64,512]{3,2,1,0:T(8,128)(2,1)S(1)}, u32[]{:S(2)}, u32[]{:S(2)}) collective-permute-start(bf16[2,2,64,512]{3,2,1,0:T(8,128)(2,1)S(1)} %bitcast.19), channel_id=1, source_target_pairs={{0,384},{128,0},{256,128},{384,256},{1,385},{129,1},{257,129},{385... | collective-permute-start | bytes 786440 | tf_op jit(solution)/shard_map/ppermute | solution.py:199
  69.6 3.9 %collective-permute-done.1.refs_3_ = bf16[2,2,64,512]{3,2,1,0:T(8,128)(2,1)S(1)} collective-permute-done((bf16[2,2,64,512]{3,2,1,0:T(8,128)(2,1)S(1)}, bf16[2,2,64,512]{3,2,1,0:T(8,128)(2,1)S(1)}, u32[]{:S(2)}, u32[]{:S(2)}) %collective-permute-start.1) | collective-permute-done | bytes 262176 | tf_op jit(solution)/shard_map/ppermute | solution.py:199
  73.5 2.0 %collective-permute-done.2.refs_4_ = bf16[2,2,64,512]{3,2,1,0:T(8,128)(2,1)S(1)} collective-permute-done((bf16[2,2,64,512]{3,2,1,0:T(8,128)(2,1)S(1)}, bf16[2,2,64,512]{3,2,1,0:T(8,128)(2,1)S(1)}, u32[]{:S(2)}, u32[]{:S(2)}) %collective-permute-start.2) | collective-permute-done | bytes 262176 | tf_op jit(solution)/shard_map/ppermute | solution.py:199
  75.5 1.6 %collective-permute-done.3.refs_5_ = bf16[2,2,64,512]{3,2,1,0:T(8,128)(2,1)S(1)} collective-permute-done((bf16[2,2,64,512]{3,2,1,0:T(8,128)(2,1)S(1)}, bf16[2,2,64,512]{3,2,1,0:T(8,128)(2,1)S(1)}, u32[]{:S(2)}, u32[]{:S(2)}) %collective-permute-start.3) | collective-permute-done | bytes 262176 | tf_op jit(solution)/shard_map/ppermute | solution.py:199
  77.1 0.0 all-to-all-done.2.refs_1_
  77.2 5.9 %shard_map.40 = bf16[512,128]{1,0:T(8,128)(2,1)S(1)} custom-call(s32[2]{0:T(128)S(1)} %pad_add_fusion.refs_1_.refs_0_, bf16[4,512,128]{2,1,0:T(8,128)(2,1)S(1)} %all-to-all-done.2.refs_1_, bf16[2,2,64,512]{3,2,1,0:T(8,128)(2,1)S(1)} %bitcast.20, bf16[2,2,64,512]{3,2,1,0:T(8,128)(2,1)S(1)} %collective-permute-done.1.refs_3_, ...), custom_call_target="tpu_custom_call" | custom-call | flops 3221225472 | bytes 2097152 | tf_op jit(solution)/shard_map/pallas_call | solution.py:211
  83.0 15.4 %all_to_all.27.in_ref = bf16[16,4,8,128]{3,2,1,0:T(8,128)(2,1)S(1)} all-to-all(bf16[16,4,8,128]{3,2,1,0:T(8,128)(2,1)S(1)} %bitcast.16), channel_id=1, replica_groups=mesh['x'=4,'core'=2,'shard'=16,'tensor'=4] {'shard'}, dimensions={0} | all-to-all | bytes 262144 | tf_op jit(solution)/shard_map/all_to_all | solution.py:219
  98.4 0.1 shard_map.41
  98.5 15.7 %all_to_all.28 = bf16[16,16,8,128]{3,2,1,0:T(8,128)(2,1)S(1)} all-to-all(bf16[16,16,8,128]{3,2,1,0:T(8,128)(2,1)S(1)} %bitcast.11), channel_id=1, replica_groups=mesh['x'=4,'core'=2,'shard'=16,'tensor'=4] {'x','tensor'}, dimensions={0} | all-to-all | bytes 1048576 | tf_op jit(solution)/shard_map/all_to_all | solution.py:223
  114.2 6.9 %collective-permute-start.4 = (bf16[4,4,16,8,128]{4,3,2,1,0:T(8,128)(2,1)S(1)}, bf16[4,4,16,8,128]{4,3,2,1,0:T(8,128)(2,1)S(1)}, u32[]{:S(2)}, u32[]{:S(2)}) collective-permute-start(bf16[4,4,16,8,128]{4,3,2,1,0:T(8,128)(2,1)S(1)} %bitcast.12), channel_id=1, source_target_pairs={{0,64},{64,0},{1,65},{65,1},{2,66},{66,2},{3,67},{67,3},{4,68},{68... | collective-permute-start | bytes 1572872 | tf_op jit(solution)/shard_map/ppermute | solution.py:226
  121.2 1.5 %collective-permute-done.4.refs_3_ = bf16[4,4,16,8,128]{4,3,2,1,0:T(8,128)(2,1)S(1)} collective-permute-done((bf16[4,4,16,8,128]{4,3,2,1,0:T(8,128)(2,1)S(1)}, bf16[4,4,16,8,128]{4,3,2,1,0:T(8,128)(2,1)S(1)}, u32[]{:S(2)}, u32[]{:S(2)}) %collective-permute-start.4) | collective-permute-done | bytes 524320 | tf_op jit(solution)/shard_map/ppermute | solution.py:226
  122.7 3.1 %shard_map.42 = bf16[64,8,512]{2,1,0:T(8,128)(2,1)} custom-call(s32[64]{0:T(128)S(1)} %copy-done.2, s32[2]{0:T(128)S(1)} %pad_add_fusion.refs_1_.refs_0_, bf16[4,4,16,8,128]{4,3,2,1,0:T(8,128)(2,1)S(1)} %bitcast.13, bf16[4,4,16,8,128]{4,3,2,1,0:T(8,128)(2,1)S(1)} %collective-permute-done.4.refs_3_), custom_call_target="tpu_custom_call" | custom-call | bytes 1048576 | tf_op jit(solution)/shard_map/pallas_call | solution.py:231
Async XLA Ops:
  0.1 0.7 copy-start.2
  0.7 1.0 copy-start
  1.8 1.0 copy-start.1
  5.1 10.5 %collective-permute-start = (bf16[80,8,512]{2,1,0:T(8,128)(2,1)S(1)}, bf16[80,8,512]{2,1,0:T(8,128)(2,1)S(1)}, u32[]{:S(2)}, u32[]{:S(2)}) collective-permute-start(bf16[80,8,512]{2,1,0:T(8,128)(2,1)S(1)} %get-tuple-element.10), channel_id=1, source_target_pairs={{0,64},{64,0},{1,65},{65,1},{2,66},{66,2},{3,67},{67,3},{4,68},{68... | collective-permute-start | bytes 1966088 | tf_op jit(solution)/shard_map/ppermute | solution.py:186
  55.4 21.7 %all-to-all-start.2 = ((bf16[4,512,128]{2,1,0:T(8,128)(2,1)}), bf16[4,512,128]{2,1,0:T(8,128)(2,1)S(1)}, u32[]{:S(2)}, u32[]{:S(2)}) async-start(bf16[4,512,128]{2,1,0:T(8,128)(2,1)} %broadcast_in_dim.8), calls=%async_computation.2 | async-start | bytes 1048576 | tf_op jit(solution)/shard_map/all_to_all | solution.py:204
  58.9 14.6 %collective-permute-start.1 = (bf16[2,2,64,512]{3,2,1,0:T(8,128)(2,1)S(1)}, bf16[2,2,64,512]{3,2,1,0:T(8,128)(2,1)S(1)}, u32[]{:S(2)}, u32[]{:S(2)}) collective-permute-start(bf16[2,2,64,512]{3,2,1,0:T(8,128)(2,1)S(1)} %bitcast.17), channel_id=1, source_target_pairs={{0,128},{128,256},{256,384},{384,0},{1,129},{129,257},{257,385},{3... | collective-permute-start | bytes 786440 | tf_op jit(solution)/shard_map/ppermute | solution.py:199
  62.2 13.3 %collective-permute-start.2 = (bf16[2,2,64,512]{3,2,1,0:T(8,128)(2,1)S(1)}, bf16[2,2,64,512]{3,2,1,0:T(8,128)(2,1)S(1)}, u32[]{:S(2)}, u32[]{:S(2)}) collective-permute-start(bf16[2,2,64,512]{3,2,1,0:T(8,128)(2,1)S(1)} %bitcast.18), channel_id=1, source_target_pairs={{0,256},{128,384},{256,0},{384,128},{1,257},{129,385},{257,1},{385... | collective-permute-start | bytes 786440 | tf_op jit(solution)/shard_map/ppermute | solution.py:199
  66.5 10.6 %collective-permute-start.3 = (bf16[2,2,64,512]{3,2,1,0:T(8,128)(2,1)S(1)}, bf16[2,2,64,512]{3,2,1,0:T(8,128)(2,1)S(1)}, u32[]{:S(2)}, u32[]{:S(2)}) collective-permute-start(bf16[2,2,64,512]{3,2,1,0:T(8,128)(2,1)S(1)} %bitcast.19), channel_id=1, source_target_pairs={{0,384},{128,0},{256,128},{384,256},{1,385},{129,1},{257,129},{385... | collective-permute-start | bytes 786440 | tf_op jit(solution)/shard_map/ppermute | solution.py:199
  114.2 8.5 %collective-permute-start.4 = (bf16[4,4,16,8,128]{4,3,2,1,0:T(8,128)(2,1)S(1)}, bf16[4,4,16,8,128]{4,3,2,1,0:T(8,128)(2,1)S(1)}, u32[]{:S(2)}, u32[]{:S(2)}) collective-permute-start(bf16[4,4,16,8,128]{4,3,2,1,0:T(8,128)(2,1)S(1)} %bitcast.12), channel_id=1, source_target_pairs={{0,64},{64,0},{1,65},{65,1},{2,66},{66,2},{3,67},{67,3},{4,68},{68... | collective-permute-start | bytes 1572872 | tf_op jit(solution)/shard_map/ppermute | solution.py:226

commit v2 on v1

v2 whole, which is shorter than its diff:
```python
import functools

import jax
import jax.numpy as jnp
from jax import lax
from jax.experimental import pallas as pl
from jax.experimental.pallas import tpu as pltpu
from jax.sharding import Mesh, PartitionSpec as P

ridge_term = 1e-06
decay_rate = 0.95
graft_floor = 1e-06
start_scale = 4.0

BF = jnp.bfloat16
F32 = jnp.float32
VMEM_LIMIT = 48 * 1024 * 1024


def call(kernel, out_shape, in_kinds, scratch=(), out_kind="v", flops=0, nbytes=1 << 20):
    kinds = {"v": pltpu.VMEM, "h": pltpu.HBM}
    single = not isinstance(out_shape, (list, tuple))
    spec = pl.BlockSpec(memory_space=kinds[out_kind])
    return pl.pallas_call(
        kernel,
        out_shape=out_shape,
        in_specs=[pl.BlockSpec(memory_space=kinds[k]) for k in in_kinds],
        out_specs=spec if single else [spec] * len(out_shape),
        scratch_shapes=list(scratch),
        compiler_params=pltpu.CompilerParams(vmem_limit_bytes=VMEM_LIMIT),
        cost_estimate=pl.CostEstimate(flops=flops, bytes_accessed=nbytes, transcendentals=0),
    )


def place_kernel(ny, nz, slot_hbm, grad_hbm, stat_hbm, keep_ref, send_ref, slots, source, grads, stats, sems):
    blocks = grad_hbm.shape[1]
    owners = ny * nz
    core = lax.axis_index("core")
    copies = [
        pltpu.make_async_copy(slot_hbm, slots, sems.at[0]),
        pltpu.make_async_copy(grad_hbm.at[0], grads.at[pl.ds(0, blocks)], sems.at[1]),
        pltpu.make_async_copy(stat_hbm, stats, sems.at[2]),
    ]
    for copy in copies:
        copy.start()
    grads[blocks] = jnp.zeros(grads.shape[1:], BF)

    def clear(place, carry):
        source[place] = blocks
        return carry

    lax.fori_loop(0, 2 * owners, clear, 0, unroll=8)
    copies[0].wait()

    def fill(block, carry):
        slot = slots[block]
        owner = slot // 2
        away = (slot % 2 + core) % 2
        source[away * owners + (owner % ny) * nz + owner // ny] = block
        return carry

    lax.fori_loop(0, blocks, fill, 0, unroll=8)
    copies[1].wait()

    def move(place, carry):
        keep_ref[place] = grads[source[place]]
        send_ref[place] = grads[source[owners + place]]
        return carry

    lax.fori_loop(0, owners, move, 0, unroll=8)
    copies[2].wait()
    tail_shape = (keep_ref.shape[0] - owners,) + keep_ref.shape[1:]
    keep_ref[owners:] = stats[core].reshape(tail_shape).astype(BF)
    send_ref[owners:] = stats[1 - core].reshape(tail_shape).astype(BF)


def quarter_kernel(nx, keep_ref, got_ref, out_ref, stat_ref):
    owners = out_ref.shape[1] * out_ref.shape[2]
    width = out_ref.shape[-1]
    core = lax.axis_index("core")
    for part in range(nx):
        cols = slice(part * width, (part + 1) * width)
        total = keep_ref[:owners, :, cols].astype(F32) + got_ref[:owners, :, cols].astype(F32)
        out_ref[part] = total.astype(BF).reshape(out_ref.shape[1:])
    half = stat_ref.shape[1] // 2
    for ref, place in ((keep_ref, core), (got_ref, 1 - core)):
        rows = pl.ds(pl.multiple_of(place * half, half), half)
        stat_ref[:, rows, :] = ref[owners:].reshape(2, half, stat_ref.shape[2])


def sum_kernel(in_ref, out_ref):
    nx, ny = in_ref.shape[:2]
    for part in range(ny):
        total = in_ref[0, part].astype(F32)
        for copy in range(1, nx):
            total = total + in_ref[copy, part].astype(F32)
        out_ref[:, part] = total.astype(BF)


def fan_kernel(in_ref, stat_ref, out_ref):
    nx = out_ref.shape[0]
    order, width = in_ref.shape
    x = lax.axis_index("x")

    def columns(side, shift):
        return stat_ref[side, :, pl.ds(pl.multiple_of(lax.rem(x + shift, nx) * width, width), width)]

    for chip in range(nx):
        out_ref[chip, :order] = in_ref[...]
    for shift in range(1, nx):
        chip = lax.rem(x - shift + nx, nx)
        for side in range(2):
            base = order + 2 * side * width
            out_ref[chip, base : base + width] = columns(side, 0)
            out_ref[chip, base + width : base + 2 * width] = columns(side, 1 if shift < nx - 1 else 2)


def dot(left, right, contract=((1,), (0,))):
    return lax.dot_general(left, right, (contract, ((), ())), preferred_element_type=F32)


def step_kernel(own_ref, got_ref, out_ref, grad_ref, stat_ref):
    nx, _, width = got_ref.shape
    order = grad_ref.shape[0]
    x = lax.axis_index("x")
    for part in range(nx):
        grad_ref[:, part * width : (part + 1) * width] = got_ref[part, :order]

    eye = (
        lax.broadcasted_iota(jnp.int32, (width, width), 0) == lax.broadcasted_iota(jnp.int32, (width, width), 1)
    ).astype(BF)

    def at(shift):
        return pl.ds(pl.multiple_of(lax.rem(x + shift, nx) * width, width), width)

    for side in range(2):
        stat_ref[side, at(0), :] = own_ref[side]
        for shift in range(1, nx):
            block = own_ref[side, :, at(shift)]
            stat_ref[side, at(shift), at(0)] = dot(eye, block, ((1,), (1,))).astype(BF)
            source = lax.rem(x + shift, nx)
            partner = shift % (nx - 1) + 1
            base = order + 2 * side * width
            stat_ref[side, at(shift), at(shift)] = got_ref[source, base : base + width]
            block = got_ref[source, base + width : base + 2 * width]
            stat_ref[side, at(shift), at(partner)] = block
            stat_ref[side, at(partner), at(shift)] = dot(eye, block, ((1,), (1,))).astype(BF)

    grad = grad_ref[...]
    row_ids = lax.broadcasted_iota(jnp.int32, (order, order), 0)
    col_ids = lax.broadcasted_iota(jnp.int32, (order, order), 1)
    diagonal = row_ids == col_ids
    roots = []
    for side in range(2):
        gram = dot(grad, grad, ((1,), (1,)) if side == 0 else ((0,), (0,)))
        shifted = decay_rate * stat_ref[side].astype(F32) + gram + jnp.where(diagonal, ridge_term, 0.0)
        delta = shifted * (-0.25 * start_scale * lax.rsqrt(jnp.sum(shifted * shifted)))
        low = delta.astype(BF)
        squared = dot(low, low)
        square = (squared + 2.5 * delta + jnp.where(diagonal, 1.5625, 0.0)).astype(BF)
        tail = (1.25 * delta + squared).astype(BF)
        fourth = dot(square, square).astype(BF)
        root = dot(fourth, tail) + 1.25 * delta + jnp.where(diagonal, 1.5625, 0.0)
        roots.append(root.astype(BF))
    half = dot(roots[0], grad).astype(BF)
    precond = dot(half, roots[1])
    count = float(order * order)
    grad32 = grad.astype(F32)
    mean_grad = jnp.sum(grad32 * grad32) / count
    mean_pre = jnp.sum(precond * precond) / count
    scale = jnp.sqrt(mean_grad) / jnp.sqrt(mean_pre + graft_floor)
    for part in range(nx):

        @pl.when(x == part)
        def _():
            out_ref[...] = (precond[:, part * width : (part + 1) * width] * scale).astype(BF)


def spread_kernel(in_ref, out_ref):
    nx, ny = out_ref.shape[:2]
    for part in range(ny):
        piece = in_ref[:, part]
        for copy in range(nx):
            out_ref[copy, part] = piece


def pick_kernel(chunks, slot_hbm, own_ref, got_ref, out_hbm, slots, out, sems):
    nx, ny, nz = own_ref.shape[:3]
    width = own_ref.shape[-1]
    blocks = out.shape[0]
    size = blocks // chunks
    core = lax.axis_index("core")
    fetch = pltpu.make_async_copy(slot_hbm, slots, sems.at[chunks])
    fetch.start()
    fetch.wait()
    copies = []
    for chunk in range(chunks):

        def move(step, carry):
            block = chunk * size + step
            slot = slots[block]
            owner = slot // 2
            y, z = owner % ny, owner // ny
            mine = slot % 2 == core
            for part in range(nx):
                out[block, :, part * width : (part + 1) * width] = jnp.where(
                    mine, own_ref[part, y, z], got_ref[part, y, z]
                )
            return carry

        lax.fori_loop(0, size, move, 0, unroll=8)
        span = pl.ds(chunk * size, size)
        copies.append(pltpu.make_async_copy(out.at[span], out_hbm.at[span], sems.at[chunk]))
        copies[-1].start()
    for copy in copies:
        copy.wait()


def shaped(shape, dtype=BF):
    return jax.ShapeDtypeStruct(shape, dtype)


def on_device(gradients, old_stats, owner_slot):
    nx, nz, ny = lax.axis_size("x"), lax.axis_size("shard"), lax.axis_size("tensor")
    blocks, rows, order = gradients.shape[1:]
    owners = ny * nz
    width = order // nx
    stat_rows = old_stats.shape[2]
    tail = 2 * stat_rows // rows
    swap = [(0, 1), (1, 0)]
    exchange = functools.partial(lax.all_to_all, split_axis=0, concat_axis=0, tiled=True)

    whole = (owners + tail, rows, order)
    keep, send = call(
        functools.partial(place_kernel, ny, nz),
        [shaped(whole), shaped(whole)],
        "hhh",
        scratch=[
            pltpu.SMEM(owner_slot.shape, jnp.int32),
            pltpu.SMEM((2 * owners,), jnp.int32),
            pltpu.VMEM((blocks + 1, rows, order), BF),
            pltpu.VMEM(old_stats.shape, F32),
            pltpu.SemaphoreType.DMA((3,)),
        ],
    )(owner_slot, gradients, old_stats)
    got = lax.ppermute(send, "core", swap)
    parts, stat = call(
        functools.partial(quarter_kernel, nx),
        [shaped((nx, ny, nz, rows, width)), shaped((2, 2 * stat_rows, order))],
        "vv",
    )(keep, got)
    parts = exchange(parts.reshape(nx * ny, nz, rows, width), ("x", "tensor"))
    summed = call(sum_kernel, shaped((nz, ny, rows, width)), "v")(parts.reshape(nx, ny, nz, rows, width))
    quarter_grad = exchange(summed, "shard").reshape(order, width)
    fanned = call(fan_kernel, shaped((nx, order + 4 * width, width)), "vv")(quarter_grad, stat)
    gathered = exchange(fanned, "x")
    update = call(
        step_kernel,
        shaped((order, width)),
        "vv",
        scratch=[pltpu.VMEM((order, order), BF), pltpu.VMEM((2, order, order), BF)],
        flops=20 * order**3,
        nbytes=2 << 20,
    )(stat, gathered)
    back = exchange(update.reshape(nz, ny, rows, width), "shard")
    spread = call(spread_kernel, shaped((nx, ny, nz, rows, width)), "v")(back)
    own = exchange(spread.reshape(nx * ny, nz, rows, width), ("x", "tensor"))
    own = own.reshape(nx, ny, nz, rows, width)
    chunks = 4
    return call(
        functools.partial(pick_kernel, chunks),
        shaped((blocks, rows, order)),
        "hvv",
        scratch=[
            pltpu.SMEM(owner_slot.shape, jnp.int32),
            pltpu.VMEM((blocks, rows, order), BF),
            pltpu.SemaphoreType.DMA((chunks + 1,)),
        ],
        out_kind="h",
    )(owner_slot, own, lax.ppermute(own, "core", swap))


def solution(mesh):
    replica, nz, ny = (mesh.shape[name] for name in ("replica", "shard", "tensor"))
    fine = Mesh(mesh.devices.reshape(replica // 2, 2, nz, ny), ("x", "core", "shard", "tensor"))
    replicas, rows = ("x", "core"), ("shard", "tensor")
    return jax.shard_map(
        on_device,
        mesh=fine,
        in_specs=(P(replicas, None, rows, None), P(rows, None, replicas, None), P()),
        out_specs=P(None, rows, None),
        check_vma=False,
    )
```

time: 126 us -> 115 us (0.913)
  blocking collectives: 69.4 us -> 83.1 us
  starting transfers between devices: 29.9 us -> 16.4 us
  waiting for transfers between devices: 10.7 us -> 3.22 us
  Pallas kernels: 12 us -> 9.16 us
    all_to_all x4 -> x5, blocking collectives: 69.4 us -> 83.1 us  [the longest x1 25.4 us: on_device(): quarter_grad = exchange(summed, 'shard').reshape(order, width)]
    ppermute x4 -> x1, starting transfers between devices: 17.7 us -> 7.61 us  [on_device(): lax.ppermute(own, 'core', swap)]
    ppermute x4 -> x1, waiting for transfers between devices: 9.02 us -> 1.51 us  [on_device(): lax.ppermute(own, 'core', swap)]
    all_to_all x1 -> x0, starting transfers between devices: 3.47 us -> none  [on_device(): lax.all_to_all(jnp.broadcast_to(quarter_grad, (nx, order, width)), 'x', s...]
    pallas_call x5 -> x6, Pallas kernels: 11.9 us -> 9.1 us  [the longest x1 4.89 us: on_device(): call(step_kernel, shaped((order, width)), 'vv', scratch=[pltpu.VMEM((orde...]
    unnamed x6 -> x8, local copies, waits for them, and re-layouts: 2.74 us -> 2.74 us
  transfers between devices with their start and end apart: 6 -> 2, of which waited for: 5 -> 2; matrix products, arithmetic and copies ran while one was open for 0% -> 0% of each run, Pallas kernels for 0% -> 0%
where the time goes in v2:
time: 115 us
  blocking collectives  83.1 us (72%)
  starting transfers between devices  16.4 us (14%)
  Pallas kernels  9.16 us (8%)
  waiting for transfers between devices  3.22 us (3%)
  local copies, waits for them, and re-layouts  2.74 us (2%)
    all_to_all x1, blocking collectives, on_device(): quarter_grad = exchange(summed, 'shard').reshape(order, width)  25.4 us
    all_to_all x1, blocking collectives, on_device(): back = exchange(update.reshape(nz, ny, rows, width), 'shard')  18.6 us
    all_to_all x1, blocking collectives, on_device(): gathered = exchange(fanned, 'x')  13.2 us
    all_to_all x1, blocking collectives, on_device(): own = exchange(spread.reshape(nx * ny, nz, rows, width), ('x', 'tensor'))  13.1 us
    all_to_all x1, blocking collectives, on_device(): parts = exchange(parts.reshape(nx * ny, nz, rows, width), ('x', 'tensor'))  12.9 us
    ppermute x1, starting transfers between devices, on_device(): got = lax.ppermute(send, 'core', swap)  8.79 us
    ppermute x1, starting transfers between devices, on_device(): lax.ppermute(own, 'core', swap)  7.61 us
    pallas_call x1, Pallas kernels, on_device(): call(step_kernel, shaped((order, width)), 'vv', scratch=[pltpu.VMEM((orde...  4.89 us
  transfers between devices with their start and end apart: 2, of which 2 were waited for; matrix products, arithmetic and copies ran while one was open for 0% of the time, Pallas kernels for 0%

profile of v2, /device:TPU:1, one launch (start us, length us, event | category | flops | bytes accessed | tf_op | source)
XLA Modules:
  0.0 114.6 jit_solution(1973702798542847281)
XLA Ops:
  0.0 0.0 copy-start
  0.0 1.0 copy-done
  1.0 0.0 copy-start.1
  1.0 1.0 copy-done.1
  2.1 0.0 copy-start.2
  2.1 0.7 copy-done.2
  2.7 1.7 %shard_map.37 = (bf16[80,8,512]{2,1,0:T(8,128)(2,1)S(1)}, bf16[80,8,512]{2,1,0:T(8,128)(2,1)S(1)}) custom-call(s32[64]{0:T(128)S(1)} %copy-done.2, bf16[1,64,8,512]{3,2,1,0:T(8,128)(2,1)S(1)} %copy-done, f32[2,2,64,512]{3,2,1,0:T(8,128)S(1)} %copy-done.1), custom_call_target="tpu_custom_call" | custom-call | bytes 1048576 | tf_op jit(solution)/shard_map/pallas_call | solution.py:234
  4.5 8.8 %collective-permute-start = (bf16[80,8,512]{2,1,0:T(8,128)(2,1)S(1)}, bf16[80,8,512]{2,1,0:T(8,128)(2,1)S(1)}, u32[]{:S(2)}, u32[]{:S(2)}) collective-permute-start(bf16[80,8,512]{2,1,0:T(8,128)(2,1)S(1)} %get-tuple-element.10), channel_id=1, source_target_pairs={{0,64},{64,0},{1,65},{65,1},{2,66},{66,2},{3,67},{67,3},{4,68},{68... | collective-permute-start | bytes 1966088 | tf_op jit(solution)/shard_map/ppermute | solution.py:246
  13.3 1.7 %collective-permute-done.got_ref = bf16[80,8,512]{2,1,0:T(8,128)(2,1)S(1)} collective-permute-done((bf16[80,8,512]{2,1,0:T(8,128)(2,1)S(1)}, bf16[80,8,512]{2,1,0:T(8,128)(2,1)S(1)}, u32[]{:S(2)}, u32[]{:S(2)}) %collective-permute-start) | collective-permute-done | bytes 655392 | tf_op jit(solution)/shard_map/ppermute | solution.py:246
  15.0 0.1 shard_map.38
  15.1 12.9 %all_to_all.25 = bf16[16,16,8,128]{3,2,1,0:T(8,128)(2,1)S(1)} all-to-all(bf16[16,16,8,128]{3,2,1,0:T(8,128)(2,1)S(1)} %bitcast.10), channel_id=1, replica_groups=mesh['x'=4,'core'=2,'shard'=16,'tensor'=4] {'x','tensor'}, dimensions={0} | all-to-all | bytes 1048576 | tf_op jit(solution)/shard_map/all_to_all | solution.py:252
  28.0 0.1 shard_map.39
  28.1 25.4 %all_to_all.26 = bf16[16,4,8,128]{3,2,1,0:T(8,128)(2,1)S(1)} all-to-all(bf16[16,4,8,128]{3,2,1,0:T(8,128)(2,1)S(1)} %shard_map.39), channel_id=1, replica_groups=mesh['x'=4,'core'=2,'shard'=16,'tensor'=4] {'shard'}, dimensions={0} | all-to-all | bytes 262144 | tf_op jit(solution)/shard_map/all_to_all | solution.py:254
  53.5 0.1 shard_map.40
  53.6 13.2 %all_to_all.27.got_ref = bf16[4,1024,128]{2,1,0:T(8,128)(2,1)S(1)} all-to-all(bf16[4,1024,128]{2,1,0:T(8,128)(2,1)S(1)} %shard_map.40), channel_id=1, replica_groups=mesh['x'=4,'core'=2,'shard'=16,'tensor'=4] {'x'}, dimensions={0} | all-to-all | bytes 2097152 | tf_op jit(solution)/shard_map/all_to_all | solution.py:256
  66.8 4.9 %shard_map.41 = bf16[512,128]{1,0:T(8,128)(2,1)S(1)} custom-call(bf16[2,128,512]{2,1,0:T(8,128)(2,1)S(1)} %get-tuple-element.11.stat_ref.own_ref, bf16[4,1024,128]{2,1,0:T(8,128)(2,1)S(1)} %all_to_all.27.got_ref), custom_call_target="tpu_custom_call" | custom-call | flops 2684354560 | bytes 2097152 | tf_op jit(solution)/shard_map/pallas_call | solution.py:257
  71.7 18.6 %all_to_all.28.in_ref = bf16[16,4,8,128]{3,2,1,0:T(8,128)(2,1)S(1)} all-to-all(bf16[16,4,8,128]{3,2,1,0:T(8,128)(2,1)S(1)} %bitcast.12), channel_id=1, replica_groups=mesh['x'=4,'core'=2,'shard'=16,'tensor'=4] {'shard'}, dimensions={0} | all-to-all | bytes 262144 | tf_op jit(solution)/shard_map/all_to_all | solution.py:265
  90.2 0.1 shard_map.42
  90.3 13.1 %all_to_all.29 = bf16[16,16,8,128]{3,2,1,0:T(8,128)(2,1)S(1)} all-to-all(bf16[16,16,8,128]{3,2,1,0:T(8,128)(2,1)S(1)} %bitcast.7), channel_id=1, replica_groups=mesh['x'=4,'core'=2,'shard'=16,'tensor'=4] {'x','tensor'}, dimensions={0} | all-to-all | bytes 1048576 | tf_op jit(solution)/shard_map/all_to_all | solution.py:267
  103.4 0.0 copy-start.3
  103.4 7.6 %collective-permute-start.1 = (bf16[4,4,16,8,128]{4,3,2,1,0:T(8,128)(2,1)S(1)}, bf16[4,4,16,8,128]{4,3,2,1,0:T(8,128)(2,1)S(1)}, u32[]{:S(2)}, u32[]{:S(2)}) collective-permute-start(bf16[4,4,16,8,128]{4,3,2,1,0:T(8,128)(2,1)S(1)} %bitcast.8), channel_id=1, source_target_pairs={{0,64},{64,0},{1,65},{65,1},{2,66},{66,2},{3,67},{67,3},{4,68},{68... | collective-permute-start | bytes 1572872 | tf_op jit(solution)/shard_map/ppermute | solution.py:280
  111.0 1.5 %collective-permute-done.1.got_ref = bf16[4,4,16,8,128]{4,3,2,1,0:T(8,128)(2,1)S(1)} collective-permute-done((bf16[4,4,16,8,128]{4,3,2,1,0:T(8,128)(2,1)S(1)}, bf16[4,4,16,8,128]{4,3,2,1,0:T(8,128)(2,1)S(1)}, u32[]{:S(2)}, u32[]{:S(2)}) %collective-permute-start.1) | collective-permute-done | bytes 524320 | tf_op jit(solution)/shard_map/ppermute | solution.py:280
  112.5 0.0 copy-done.3
  112.5 2.1 %shard_map.43 = bf16[64,8,512]{2,1,0:T(8,128)(2,1)} custom-call(s32[64]{0:T(128)S(1)} %copy-done.3, bf16[4,4,16,8,128]{4,3,2,1,0:T(8,128)(2,1)S(1)} %bitcast.9, bf16[4,4,16,8,128]{4,3,2,1,0:T(8,128)(2,1)S(1)} %collective-permute-done.1.got_ref), custom_call_target="tpu_custom_call" | custom-call | bytes 1048576 | tf_op jit(solution)/shard_map/pallas_call | solution.py:270
Async XLA Ops:
  0.0 1.0 copy-start
  1.0 1.0 copy-start.1
  2.1 0.7 copy-start.2
  4.5 10.5 %collective-permute-start = (bf16[80,8,512]{2,1,0:T(8,128)(2,1)S(1)}, bf16[80,8,512]{2,1,0:T(8,128)(2,1)S(1)}, u32[]{:S(2)}, u32[]{:S(2)}) collective-permute-start(bf16[80,8,512]{2,1,0:T(8,128)(2,1)S(1)} %get-tuple-element.10), channel_id=1, source_target_pairs={{0,64},{64,0},{1,65},{65,1},{2,66},{66,2},{3,67},{67,3},{4,68},{68... | collective-permute-start | bytes 1966088 | tf_op jit(solution)/shard_map/ppermute | solution.py:246
  103.4 9.1 %copy-start.3 = (s32[64]{0:T(128)S(1)}, s32[64]{0:T(128)}, u32[]{:S(2)}) copy-start(s32[64]{0:T(128)} %slot_hbm.3) | copy-start | bytes 772
  103.4 9.1 %collective-permute-start.1 = (bf16[4,4,16,8,128]{4,3,2,1,0:T(8,128)(2,1)S(1)}, bf16[4,4,16,8,128]{4,3,2,1,0:T(8,128)(2,1)S(1)}, u32[]{:S(2)}, u32[]{:S(2)}) collective-permute-start(bf16[4,4,16,8,128]{4,3,2,1,0:T(8,128)(2,1)S(1)} %bitcast.8), channel_id=1, source_target_pairs={{0,64},{64,0},{1,65},{65,1},{2,66},{66,2},{3,67},{67,3},{4,68},{68... | collective-permute-start | bytes 1572872 | tf_op jit(solution)/shard_map/ppermute | solution.py:280

commit v3 on v2

--- a/solution.py
+++ b/solution.py
@@ -32,46 +32,43 @@
     )
 
 
-def place_kernel(ny, nz, slot_hbm, grad_hbm, stat_hbm, keep_ref, send_ref, slots, source, grads, stats, sems):
-    blocks = grad_hbm.shape[1]
+def place_kernel(ny, nz, chunks, slot_hbm, grad_hbm, stat_hbm, keep_ref, send_ref, slots, grads, stats, sems):
+    blocks = grads.shape[0]
     owners = ny * nz
+    dump = keep_ref.shape[0] - 1
+    size = blocks // chunks
     core = lax.axis_index("core")
-    copies = [
-        pltpu.make_async_copy(slot_hbm, slots, sems.at[0]),
-        pltpu.make_async_copy(grad_hbm.at[0], grads.at[pl.ds(0, blocks)], sems.at[1]),
-        pltpu.make_async_copy(stat_hbm, stats, sems.at[2]),
-    ]
-    for copy in copies:
-        copy.start()
-    grads[blocks] = jnp.zeros(grads.shape[1:], BF)
-
-    def clear(place, carry):
-        source[place] = blocks
-        return carry
-
-    lax.fori_loop(0, 2 * owners, clear, 0, unroll=8)
-    copies[0].wait()
-
-    def fill(block, carry):
-        slot = slots[block]
-        owner = slot // 2
-        away = (slot % 2 + core) % 2
-        source[away * owners + (owner % ny) * nz + owner // ny] = block
-        return carry
-
-    lax.fori_loop(0, blocks, fill, 0, unroll=8)
-    copies[1].wait()
-
-    def move(place, carry):
-        keep_ref[place] = grads[source[place]]
-        send_ref[place] = grads[source[owners + place]]
-        return carry
-
-    lax.fori_loop(0, owners, move, 0, unroll=8)
-    copies[2].wait()
-    tail_shape = (keep_ref.shape[0] - owners,) + keep_ref.shape[1:]
-    keep_ref[owners:] = stats[core].reshape(tail_shape).astype(BF)
-    send_ref[owners:] = stats[1 - core].reshape(tail_shape).astype(BF)
+    fetch = pltpu.make_async_copy(slot_hbm, slots, sems.at[chunks])
+    fetch.start()
+    copies = []
+    for chunk in range(chunks):
+        span = pl.ds(chunk * size, size)
+        copies.append(pltpu.make_async_copy(grad_hbm.at[0, span], grads.at[span], sems.at[chunk]))
+        copies[-1].start()
+    fetch_stats = pltpu.make_async_copy(stat_hbm, stats, sems.at[chunks + 1])
+    fetch_stats.start()
+    keep_ref[:owners] = jnp.zeros((owners,) + keep_ref.shape[1:], BF)
+    send_ref[:owners] = jnp.zeros((owners,) + keep_ref.shape[1:], BF)
+    fetch.wait()
+    for chunk in range(chunks):
+        copies[chunk].wait()
+
+        def move(step, carry):
+            block = chunk * size + step
+            slot = slots[block]
+            owner = slot // 2
+            place = (owner % ny) * nz + owner // ny
+            mine = slot % 2 == core
+            tile = grads[block]
+            keep_ref[jnp.where(mine, place, dump)] = tile
+            send_ref[jnp.where(mine, dump, place)] = tile
+            return carry
+
+        lax.fori_loop(0, size, move, 0, unroll=8)
+    fetch_stats.wait()
+    tail_shape = (dump - owners,) + keep_ref.shape[1:]
+    keep_ref[owners:dump] = stats[core].reshape(tail_shape).astype(BF)
+    send_ref[owners:dump] = stats[1 - core].reshape(tail_shape).astype(BF)
 
 
 def quarter_kernel(nx, keep_ref, got_ref, out_ref, stat_ref):
@@ -85,7 +82,7 @@
     half = stat_ref.shape[1] // 2
     for ref, place in ((keep_ref, core), (got_ref, 1 - core)):
         rows = pl.ds(pl.multiple_of(place * half, half), half)
-        stat_ref[:, rows, :] = ref[owners:].reshape(2, half, stat_ref.shape[2])
+        stat_ref[:, rows, :] = ref[owners:-1].reshape(2, half, stat_ref.shape[2])
 
 
 def sum_kernel(in_ref, out_ref):
@@ -150,18 +147,23 @@
     row_ids = lax.broadcasted_iota(jnp.int32, (order, order), 0)
     col_ids = lax.broadcasted_iota(jnp.int32, (order, order), 1)
     diagonal = row_ids == col_ids
-    roots = []
-    for side in range(2):
-        gram = dot(grad, grad, ((1,), (1,)) if side == 0 else ((0,), (0,)))
-        shifted = decay_rate * stat_ref[side].astype(F32) + gram + jnp.where(diagonal, ridge_term, 0.0)
-        delta = shifted * (-0.25 * start_scale * lax.rsqrt(jnp.sum(shifted * shifted)))
-        low = delta.astype(BF)
-        squared = dot(low, low)
-        square = (squared + 2.5 * delta + jnp.where(diagonal, 1.5625, 0.0)).astype(BF)
-        tail = (1.25 * delta + squared).astype(BF)
-        fourth = dot(square, square).astype(BF)
-        root = dot(fourth, tail) + 1.25 * delta + jnp.where(diagonal, 1.5625, 0.0)
-        roots.append(root.astype(BF))
+    sides = range(2)
+    grams = [dot(grad, grad, ((1,), (1,))), dot(grad, grad, ((0,), (0,)))]
+    deltas = []
+    for side in sides:
+        shifted = decay_rate * stat_ref[side].astype(F32) + grams[side] + jnp.where(diagonal, ridge_term, 0.0)
+        deltas.append(shifted * (-0.25 * start_scale * lax.rsqrt(jnp.sum(shifted * shifted))))
+    lows = [delta.astype(BF) for delta in deltas]
+    squares = [dot(low, low) for low in lows]
+    seconds = [
+        (squares[side] + 2.5 * deltas[side] + jnp.where(diagonal, 1.5625, 0.0)).astype(BF) for side in sides
+    ]
+    tails = [(1.25 * deltas[side] + squares[side]).astype(BF) for side in sides]
+    fourths = [dot(second, second).astype(BF) for second in seconds]
+    roots = [
+        (dot(fourths[side], tails[side]) + 1.25 * deltas[side] + jnp.where(diagonal, 1.5625, 0.0)).astype(BF)
+        for side in sides
+    ]
     half = dot(roots[0], grad).astype(BF)
     precond = dot(half, roots[1])
     count = float(order * order)
@@ -184,13 +186,13 @@
             out_ref[copy, part] = piece
 
 
-def pick_kernel(chunks, slot_hbm, own_ref, got_ref, out_hbm, slots, out, sems):
+def pick_kernel(chunks, slot_ref, own_ref, got_ref, out_hbm, slots, out, sems):
     nx, ny, nz = own_ref.shape[:3]
     width = own_ref.shape[-1]
     blocks = out.shape[0]
     size = blocks // chunks
     core = lax.axis_index("core")
-    fetch = pltpu.make_async_copy(slot_hbm, slots, sems.at[chunks])
+    fetch = pltpu.make_async_copy(slot_ref, slots, sems.at[chunks])
     fetch.start()
     fetch.wait()
     copies = []
@@ -230,19 +232,19 @@
     swap = [(0, 1), (1, 0)]
     exchange = functools.partial(lax.all_to_all, split_axis=0, concat_axis=0, tiled=True)
 
-    whole = (owners + tail, rows, order)
+    whole = (owners + tail + 1, rows, order)
+    chunks = 4
     keep, send = call(
-        functools.partial(place_kernel, ny, nz),
+        functools.partial(place_kernel, ny, nz, chunks),
         [shaped(whole), shaped(whole)],
         "hhh",
         scratch=[
             pltpu.SMEM(owner_slot.shape, jnp.int32),
-            pltpu.SMEM((2 * owners,), jnp.int32),
-            pltpu.VMEM((blocks + 1, rows, order), BF),
+            pltpu.VMEM((blocks, rows, order), BF),
             pltpu.VMEM(old_stats.shape, F32),
-            pltpu.SemaphoreType.DMA((3,)),
+            pltpu.SemaphoreType.DMA((chunks + 2,)),
         ],
-    )(owner_slot, gradients, old_stats)
+    )(*(pltpu.with_memory_space_constraint(array, pltpu.HBM) for array in (owner_slot, gradients, old_stats)))
     got = lax.ppermute(send, "core", swap)
     parts, stat = call(
         functools.partial(quarter_kernel, nx),
@@ -266,11 +268,10 @@
     spread = call(spread_kernel, shaped((nx, ny, nz, rows, width)), "v")(back)
     own = exchange(spread.reshape(nx * ny, nz, rows, width), ("x", "tensor"))
     own = own.reshape(nx, ny, nz, rows, width)
-    chunks = 4
     return call(
         functools.partial(pick_kernel, chunks),
         shaped((blocks, rows, order)),
-        "hvv",
+        "vvv",
         scratch=[
             pltpu.SMEM(owner_slot.shape, jnp.int32),
             pltpu.VMEM((blocks, rows, order), BF),

time: 115 us -> 112 us (0.974)
  local copies, waits for them, and re-layouts: 2.74 us -> 0.01 us
    unnamed x8 -> x2, local copies, waits for them, and re-layouts: 2.74 us -> 0.01 us
where the time goes in v3:
time: 112 us; the launch traced here: 111 us
  blocking collectives  83 us (74%)
  starting transfers between devices  16.5 us (15%)
  Pallas kernels  8.67 us (8%)
  waiting for transfers between devices  3.23 us (3%)
    all_to_all x1, blocking collectives, on_device(): quarter_grad = exchange(summed, 'shard').reshape(order, width)  25.4 us
    all_to_all x1, blocking collectives, on_device(): back = exchange(update.reshape(nz, ny, rows, width), 'shard')  18.6 us
    all_to_all x1, blocking collectives, on_device(): gathered = exchange(fanned, 'x')  13.2 us
    all_to_all x1, blocking collectives, on_device(): own = exchange(spread.reshape(nx * ny, nz, rows, width), ('x', 'tensor'))  13 us
    all_to_all x1, blocking collectives, on_device(): parts = exchange(parts.reshape(nx * ny, nz, rows, width), ('x', 'tensor'))  12.9 us
    ppermute x1, starting transfers between devices, on_device(): got = lax.ppermute(send, 'core', swap)  8.79 us
    ppermute x1, starting transfers between devices, on_device(): lax.ppermute(own, 'core', swap)  7.7 us
    pallas_call x1, Pallas kernels, on_device(): call(step_kernel, shaped((order, width)), 'vv', scratch=[pltpu.VMEM((orde...  4.36 us
  transfers between devices with their start and end apart: 2, of which 2 were waited for; matrix products, arithmetic and copies ran while one was open for 0% of the time, Pallas kernels for 0%

profile of v3, /device:TPU:1, one launch (start us, length us, event | category | flops | bytes accessed | tf_op | source)
XLA Modules:
  0.0 111.4 jit_solution(17642362773432242549)
XLA Ops:
  0.0 1.8 %shard_map.37 = (bf16[81,8,512]{2,1,0:T(8,128)(2,1)S(1)}, bf16[81,8,512]{2,1,0:T(8,128)(2,1)S(1)}) custom-call(s32[64]{0:T(128)} %slot_ref.1, bf16[1,64,8,512]{3,2,1,0:T(8,128)(2,1)} %grad_hbm.1, f32[2,2,64,512]{3,2,1,0:T(8,128)} %stat_hbm.1), custom_call_target="tpu_custom_call" | custom-call | bytes 1048576 | tf_op jit(solution)/shard_map/pallas_call | solution.py:237
  1.8 8.8 %collective-permute-start = (bf16[81,8,512]{2,1,0:T(8,128)(2,1)S(1)}, bf16[81,8,512]{2,1,0:T(8,128)(2,1)S(1)}, u32[]{:S(2)}, u32[]{:S(2)}) collective-permute-start(bf16[81,8,512]{2,1,0:T(8,128)(2,1)S(1)} %get-tuple-element.10), channel_id=1, source_target_pairs={{0,64},{64,0},{1,65},{65,1},{2,66},{66,2},{3,67},{67,3},{4,68},{68... | collective-permute-start | bytes 1990664 | tf_op jit(solution)/shard_map/ppermute | solution.py:248
  10.6 1.7 %collective-permute-done.got_ref = bf16[81,8,512]{2,1,0:T(8,128)(2,1)S(1)} collective-permute-done((bf16[81,8,512]{2,1,0:T(8,128)(2,1)S(1)}, bf16[81,8,512]{2,1,0:T(8,128)(2,1)S(1)}, u32[]{:S(2)}, u32[]{:S(2)}) %collective-permute-start) | collective-permute-done | bytes 663584 | tf_op jit(solution)/shard_map/ppermute | solution.py:248
  12.3 0.1 shard_map.38
  12.4 12.9 %all_to_all.25 = bf16[16,16,8,128]{3,2,1,0:T(8,128)(2,1)S(1)} all-to-all(bf16[16,16,8,128]{3,2,1,0:T(8,128)(2,1)S(1)} %bitcast.10), channel_id=1, replica_groups=mesh['x'=4,'core'=2,'shard'=16,'tensor'=4] {'x','tensor'}, dimensions={0} | all-to-all | bytes 1048576 | tf_op jit(solution)/shard_map/all_to_all | solution.py:254
  25.3 0.1 shard_map.39
  25.4 25.4 %all_to_all.26 = bf16[16,4,8,128]{3,2,1,0:T(8,128)(2,1)S(1)} all-to-all(bf16[16,4,8,128]{3,2,1,0:T(8,128)(2,1)S(1)} %shard_map.39), channel_id=1, replica_groups=mesh['x'=4,'core'=2,'shard'=16,'tensor'=4] {'shard'}, dimensions={0} | all-to-all | bytes 262144 | tf_op jit(solution)/shard_map/all_to_all | solution.py:256
  50.8 0.1 shard_map.40
  50.9 13.2 %all_to_all.27.got_ref = bf16[4,1024,128]{2,1,0:T(8,128)(2,1)S(1)} all-to-all(bf16[4,1024,128]{2,1,0:T(8,128)(2,1)S(1)} %shard_map.40), channel_id=1, replica_groups=mesh['x'=4,'core'=2,'shard'=16,'tensor'=4] {'x'}, dimensions={0} | all-to-all | bytes 2097152 | tf_op jit(solution)/shard_map/all_to_all | solution.py:258
  64.1 4.4 %shard_map.41 = bf16[512,128]{1,0:T(8,128)(2,1)S(1)} custom-call(bf16[2,128,512]{2,1,0:T(8,128)(2,1)S(1)} %get-tuple-element.11.stat_ref.own_ref, bf16[4,1024,128]{2,1,0:T(8,128)(2,1)S(1)} %all_to_all.27.got_ref), custom_call_target="tpu_custom_call" | custom-call | flops 2684354560 | bytes 2097152 | tf_op jit(solution)/shard_map/pallas_call | solution.py:259
  68.5 18.6 %all_to_all.28.in_ref = bf16[16,4,8,128]{3,2,1,0:T(8,128)(2,1)S(1)} all-to-all(bf16[16,4,8,128]{3,2,1,0:T(8,128)(2,1)S(1)} %bitcast.12), channel_id=1, replica_groups=mesh['x'=4,'core'=2,'shard'=16,'tensor'=4] {'shard'}, dimensions={0} | all-to-all | bytes 262144 | tf_op jit(solution)/shard_map/all_to_all | solution.py:267
  87.0 0.1 shard_map.42
  87.1 13.0 %all_to_all.29 = bf16[16,16,8,128]{3,2,1,0:T(8,128)(2,1)S(1)} all-to-all(bf16[16,16,8,128]{3,2,1,0:T(8,128)(2,1)S(1)} %bitcast.7), channel_id=1, replica_groups=mesh['x'=4,'core'=2,'shard'=16,'tensor'=4] {'x','tensor'}, dimensions={0} | all-to-all | bytes 1048576 | tf_op jit(solution)/shard_map/all_to_all | solution.py:269
  100.1 0.0 copy-start
  100.1 7.7 %collective-permute-start.1 = (bf16[4,4,16,8,128]{4,3,2,1,0:T(8,128)(2,1)S(1)}, bf16[4,4,16,8,128]{4,3,2,1,0:T(8,128)(2,1)S(1)}, u32[]{:S(2)}, u32[]{:S(2)}) collective-permute-start(bf16[4,4,16,8,128]{4,3,2,1,0:T(8,128)(2,1)S(1)} %bitcast.8), channel_id=1, source_target_pairs={{0,64},{64,0},{1,65},{65,1},{2,66},{66,2},{3,67},{67,3},{4,68},{68... | collective-permute-start | bytes 1572872 | tf_op jit(solution)/shard_map/ppermute | solution.py:281
  107.8 1.5 %collective-permute-done.1.got_ref = bf16[4,4,16,8,128]{4,3,2,1,0:T(8,128)(2,1)S(1)} collective-permute-done((bf16[4,4,16,8,128]{4,3,2,1,0:T(8,128)(2,1)S(1)}, bf16[4,4,16,8,128]{4,3,2,1,0:T(8,128)(2,1)S(1)}, u32[]{:S(2)}, u32[]{:S(2)}) %collective-permute-start.1) | collective-permute-done | bytes 524320 | tf_op jit(solution)/shard_map/ppermute | solution.py:281
  109.3 0.0 copy-done
  109.3 2.1 %shard_map.43 = bf16[64,8,512]{2,1,0:T(8,128)(2,1)} custom-call(s32[64]{0:T(128)S(1)} %copy-done, bf16[4,4,16,8,128]{4,3,2,1,0:T(8,128)(2,1)S(1)} %bitcast.9, bf16[4,4,16,8,128]{4,3,2,1,0:T(8,128)(2,1)S(1)} %collective-permute-done.1.got_ref), custom_call_target="tpu_custom_call" | custom-call | bytes 1048576 | tf_op jit(solution)/shard_map/pallas_call | solution.py:271
Async XLA Ops:
  1.8 10.5 %collective-permute-start = (bf16[81,8,512]{2,1,0:T(8,128)(2,1)S(1)}, bf16[81,8,512]{2,1,0:T(8,128)(2,1)S(1)}, u32[]{:S(2)}, u32[]{:S(2)}) collective-permute-start(bf16[81,8,512]{2,1,0:T(8,128)(2,1)S(1)} %get-tuple-element.10), channel_id=1, source_target_pairs={{0,64},{64,0},{1,65},{65,1},{2,66},{66,2},{3,67},{67,3},{4,68},{68... | collective-permute-start | bytes 1990664 | tf_op jit(solution)/shard_map/ppermute | solution.py:248
  100.1 9.2 %copy-start = (s32[64]{0:T(128)S(1)}, s32[64]{0:T(128)}, u32[]{:S(2)}) copy-start(s32[64]{0:T(128)} %slot_ref.1) | copy-start | bytes 772
  100.1 9.2 %collective-permute-start.1 = (bf16[4,4,16,8,128]{4,3,2,1,0:T(8,128)(2,1)S(1)}, bf16[4,4,16,8,128]{4,3,2,1,0:T(8,128)(2,1)S(1)}, u32[]{:S(2)}, u32[]{:S(2)}) collective-permute-start(bf16[4,4,16,8,128]{4,3,2,1,0:T(8,128)(2,1)S(1)} %bitcast.8), channel_id=1, source_target_pairs={{0,64},{64,0},{1,65},{65,1},{2,66},{66,2},{3,67},{67,3},{4,68},{68... | collective-permute-start | bytes 1572872 | tf_op jit(solution)/shard_map/ppermute | solution.py:281

commit v4 on v3

v4 whole, which is shorter than its diff:
```python
import functools

import jax
import jax.numpy as jnp
from jax import lax
from jax.experimental import pallas as pl
from jax.experimental.pallas import tpu as pltpu
from jax.sharding import Mesh, PartitionSpec as P

ridge_term = 1e-06
decay_rate = 0.95
graft_floor = 1e-06
start_scale = 4.0

BF = jnp.bfloat16
F32 = jnp.float32
VMEM_LIMIT = 48 * 1024 * 1024


def call(kernel, out_shape, in_kinds, scratch=(), out_kind="v", flops=0, nbytes=1 << 20):
    kinds = {"v": pltpu.VMEM, "h": pltpu.HBM}
    single = not isinstance(out_shape, (list, tuple))
    spec = pl.BlockSpec(memory_space=kinds[out_kind])
    return pl.pallas_call(
        kernel,
        out_shape=out_shape,
        in_specs=[pl.BlockSpec(memory_space=kinds[k]) for k in in_kinds],
        out_specs=spec if single else [spec] * len(out_shape),
        scratch_shapes=list(scratch),
        compiler_params=pltpu.CompilerParams(vmem_limit_bytes=VMEM_LIMIT),
        cost_estimate=pl.CostEstimate(flops=flops, bytes_accessed=nbytes, transcendentals=0),
    )


def split(slot, ny):
    owner = slot >> 1
    return owner & (ny - 1), owner >> (ny.bit_length() - 1), slot & 1


def place_kernel(ny, nz, chunks, slot_hbm, grad_hbm, stat_hbm, keep_ref, send_ref, slots, grads, stats, sems):
    blocks = grads.shape[0]
    owners = ny * nz
    dump = keep_ref.shape[0] - 1
    size = blocks // chunks
    core = lax.axis_index("core")
    fetch = pltpu.make_async_copy(slot_hbm, slots, sems.at[chunks])
    fetch.start()
    copies = []
    for chunk in range(chunks):
        span = pl.ds(chunk * size, size)
        copies.append(pltpu.make_async_copy(grad_hbm.at[0, span], grads.at[span], sems.at[chunk]))
        copies[-1].start()
    fetch_stats = pltpu.make_async_copy(stat_hbm, stats, sems.at[chunks + 1])
    fetch_stats.start()
    keep_ref[:owners] = jnp.zeros((owners,) + keep_ref.shape[1:], BF)
    send_ref[:owners] = jnp.zeros((owners,) + keep_ref.shape[1:], BF)
    fetch.wait()
    for chunk in range(chunks):
        copies[chunk].wait()

        def move(step, carry):
            block = chunk * size + step
            y, z, part = split(slots[block], ny)
            place = y * nz + z
            mine = part == core
            tile = grads[block]
            keep_ref[jnp.where(mine, place, dump)] = tile
            send_ref[jnp.where(mine, dump, place)] = tile
            return carry

        lax.fori_loop(0, size, move, 0, unroll=8)
    fetch_stats.wait()
    tail_shape = (dump - owners,) + keep_ref.shape[1:]
    keep_ref[owners:dump] = stats[core].reshape(tail_shape).astype(BF)
    send_ref[owners:dump] = stats[1 - core].reshape(tail_shape).astype(BF)


def quarter_kernel(nx, keep_ref, got_ref, out_ref, stat_ref):
    owners = out_ref.shape[1] * out_ref.shape[2]
    width = out_ref.shape[-1]
    core = lax.axis_index("core")
    for part in range(nx):
        cols = slice(part * width, (part + 1) * width)
        total = keep_ref[:owners, :, cols].astype(F32) + got_ref[:owners, :, cols].astype(F32)
        out_ref[part] = total.astype(BF).reshape(out_ref.shape[1:])
    half = stat_ref.shape[1] // 2
    for ref, place in ((keep_ref, core), (got_ref, 1 - core)):
        rows = pl.ds(pl.multiple_of(place * half, half), half)
        stat_ref[:, rows, :] = ref[owners:-1].reshape(2, half, stat_ref.shape[2])


def sum_kernel(in_ref, out_ref):
    nx, ny = in_ref.shape[:2]
    for part in range(ny):
        total = in_ref[0, part].astype(F32)
        for copy in range(1, nx):
            total = total + in_ref[copy, part].astype(F32)
        out_ref[:, part] = total.astype(BF)


def fan_stats(stat_ref, out_ref, base):
    nx, _, width = out_ref.shape
    x = lax.axis_index("x")

    def columns(side, shift):
        return stat_ref[side, :, pl.ds(pl.multiple_of(lax.rem(x + shift, nx) * width, width), width)]

    for shift in range(1, nx):
        chip = lax.rem(x - shift + nx, nx)
        for side in range(2):
            start = base + 2 * side * width
            out_ref[chip, start : start + width] = columns(side, 0)
            out_ref[chip, start + width : start + 2 * width] = columns(side, 1 if shift < nx - 1 else 2)


def fan_stats_kernel(stat_ref, out_ref):
    fan_stats(stat_ref, out_ref, 0)


def fan_grad_kernel(in_ref, out_ref):
    for chip in range(out_ref.shape[0]):
        out_ref[chip] = in_ref[...]


def fan_both_kernel(in_ref, stat_ref, out_ref):
    order = in_ref.shape[0]
    for chip in range(out_ref.shape[0]):
        out_ref[chip, :order] = in_ref[...]
    fan_stats(stat_ref, out_ref, order)


def dot(left, right, contract=((1,), (0,))):
    return lax.dot_general(left, right, (contract, ((), ())), preferred_element_type=F32)


def step_kernel(
    first,
    own_ref,
    got_ref,
    got_stat_ref,
    out_ref,
    grad_ref,
    stat_ref,
    shift_ref,
    low_ref,
    second_ref,
    tail_ref,
    root_ref,
    pre_ref,
):
    nx, _, width = got_ref.shape
    order = grad_ref.shape[0]
    x = lax.axis_index("x")
    for part in range(nx):
        grad_ref[:, part * width : (part + 1) * width] = got_ref[part, :order]

    def at(shift):
        return pl.ds(pl.multiple_of(lax.rem(x + shift, nx) * width, width), width)

    for side in range(2):
        stat_ref[side, at(0), :] = own_ref[side]
        for shift in range(1, nx):
            block = own_ref[side, :, at(shift)]
            stat_ref[side, at(shift), at(0)] = block.T
            source = lax.rem(x + shift, nx)
            partner = shift % (nx - 1) + 1
            base = first + 2 * side * width
            stat_ref[side, at(shift), at(shift)] = got_stat_ref[source, base : base + width]
            block = got_stat_ref[source, base + width : base + 2 * width]
            stat_ref[side, at(shift), at(partner)] = block
            stat_ref[side, at(partner), at(shift)] = block.T

    diagonal = lax.broadcasted_iota(jnp.int32, (order, order), 0) == lax.broadcasted_iota(
        jnp.int32, (order, order), 1
    )

    def with_diagonal(value, amount):
        return value + jnp.where(diagonal, amount, 0.0)

    scales = []
    for side in range(2):
        gram = dot(grad_ref[...], grad_ref[...], ((1 - side,), (1 - side,)))
        shifted = with_diagonal(gram + decay_rate * stat_ref[side].astype(F32), ridge_term)
        shift_ref[side] = shifted
        scales.append(-0.25 * start_scale * lax.rsqrt(jnp.sum(shifted * shifted)))
    for side in range(2):
        low_ref[side] = (shift_ref[side] * scales[side]).astype(BF)
    for side in range(2):
        squared = dot(low_ref[side], low_ref[side])
        second_ref[side] = with_diagonal(squared + shift_ref[side] * (2.5 * scales[side]), 1.5625).astype(BF)
        tail_ref[side] = (squared + shift_ref[side] * (1.25 * scales[side])).astype(BF)

    def root(side):
        fourth = dot(second_ref[side], second_ref[side]).astype(BF)
        value = dot(fourth, tail_ref[side]) + shift_ref[side] * (1.25 * scales[side])
        return with_diagonal(value, 1.5625).astype(BF)

    root_ref[...] = root(1)
    half = dot(root(0), grad_ref[...]).astype(BF)
    precond = dot(half, root_ref[...])
    pre_ref[...] = precond
    grad32 = grad_ref[...].astype(F32)
    count = float(order * order)
    mean_grad = jnp.sum(grad32 * grad32) / count
    mean_pre = jnp.sum(precond * precond) / count
    scale = jnp.sqrt(mean_grad) / jnp.sqrt(mean_pre + graft_floor)
    out_ref[...] = (pre_ref[:, at(0)] * scale).astype(BF)


def spread_kernel(in_ref, out_ref):
    nx, ny = out_ref.shape[:2]
    for part in range(ny):
        piece = in_ref[:, part]
        for copy in range(nx):
            out_ref[copy, part] = piece


def pick_kernel(slot_ref, own_ref, got_ref, out_hbm, slots, out, sems):
    nx, ny = own_ref.shape[:2]
    width = own_ref.shape[-1]
    core = lax.axis_index("core")
    fetch = pltpu.make_async_copy(slot_ref, slots, sems.at[0])
    fetch.start()
    fetch.wait()

    def move(block, carry):
        y, z, place = split(slots[block], ny)
        mine = place == core
        for part in range(nx):
            out[block, :, part * width : (part + 1) * width] = jnp.where(
                mine, own_ref[part, y, z], got_ref[part, y, z]
            )
        return carry

    lax.fori_loop(0, out.shape[0], move, 0, unroll=8)
    store = pltpu.make_async_copy(out, out_hbm, sems.at[1])
    store.start()
    store.wait()


def shaped(shape, dtype=BF):
    return jax.ShapeDtypeStruct(shape, dtype)


def on_device(gradients, old_stats, owner_slot):
    nx, nz, ny = lax.axis_size("x"), lax.axis_size("shard"), lax.axis_size("tensor")
    blocks, rows, order = gradients.shape[1:]
    owners = ny * nz
    width = order // nx
    stat_rows = old_stats.shape[2]
    tail = 2 * stat_rows // rows
    swap = [(0, 1), (1, 0)]
    exchange = functools.partial(lax.all_to_all, split_axis=0, concat_axis=0, tiled=True)

    whole = (owners + tail + 1, rows, order)
    chunks = 2
    keep, send = call(
        functools.partial(place_kernel, ny, nz, chunks),
        [shaped(whole), shaped(whole)],
        "hhh",
        scratch=[
            pltpu.SMEM(owner_slot.shape, jnp.int32),
            pltpu.VMEM((blocks, rows, order), BF),
            pltpu.VMEM(old_stats.shape, F32),
            pltpu.SemaphoreType.DMA((chunks + 2,)),
        ],
    )(*(pltpu.with_memory_space_constraint(array, pltpu.HBM) for array in (owner_slot, gradients, old_stats)))
    got = lax.ppermute(send, "core", swap)
    parts, stat = call(
        functools.partial(quarter_kernel, nx),
        [shaped((nx, ny, nz, rows, width)), shaped((2, 2 * stat_rows, order))],
        "vv",
    )(keep, got)

    def quarter_of(pieces):
        pieces = exchange(pieces.reshape(nx * ny, nz, rows, width), ("x", "tensor")).reshape(pieces.shape)
        pieces = call(sum_kernel, shaped((nz, ny, rows, width)), "v")(pieces)
        return exchange(pieces, "shard").reshape(order, width)

    def step(first, *arrays):
        return call(
            functools.partial(step_kernel, first),
            shaped((order, width)),
            "vvv",
            scratch=[
                pltpu.VMEM((order, order), BF),
                pltpu.VMEM((2, order, order), BF),
                pltpu.VMEM((2, order, order), F32),
                pltpu.VMEM((2, order, order), BF),
                pltpu.VMEM((2, order, order), BF),
                pltpu.VMEM((2, order, order), BF),
                pltpu.VMEM((order, order), BF),
                pltpu.VMEM((order, order), F32),
            ],
            flops=20 * order**3,
            nbytes=2 << 20,
        )(*arrays)

    def stats_late(pieces, stat):
        whole_shape = shaped((nx, order + 4 * width, width))
        both = exchange(call(fan_both_kernel, whole_shape, "vv")(quarter_of(pieces), stat), "x")
        return step(order, stat, both, both)

    def stats_early(pieces, stat):
        got_stat = exchange(call(fan_stats_kernel, shaped((nx, 4 * width, width)), "v")(stat), "x")
        pieces, got_stat = lax.optimization_barrier((pieces, got_stat))
        quarters = call(fan_grad_kernel, shaped((nx, order, width)), "v")(quarter_of(pieces))
        return step(0, stat, exchange(quarters, "x"), got_stat)

    update = lax.cond(lax.axis_index("core") == 0, stats_late, stats_early, parts, stat)
    back = exchange(update.reshape(nz, ny, rows, width), "shard")
    spread = call(spread_kernel, shaped((nx, ny, nz, rows, width)), "v")(back)
    own = exchange(spread.reshape(nx * ny, nz, rows, width), ("x", "tensor"))
    own = own.reshape(nx, ny, nz, rows, width)
    return call(
        pick_kernel,
        shaped((blocks, rows, order)),
        "vvv",
        scratch=[
            pltpu.SMEM(owner_slot.shape, jnp.int32),
            pltpu.VMEM((blocks, rows, order), BF),
            pltpu.SemaphoreType.DMA((2,)),
        ],
        out_kind="h",
    )(owner_slot, own, lax.ppermute(own, "core", swap))


def solution(mesh):
    replica, nz, ny = (mesh.shape[name] for name in ("replica", "shard", "tensor"))
    fine = Mesh(mesh.devices.reshape(replica // 2, 2, nz, ny), ("x", "core", "shard", "tensor"))
    replicas, rows = ("x", "core"), ("shard", "tensor")
    return jax.shard_map(
        on_device,
        mesh=fine,
        in_specs=(P(replicas, None, rows, None), P(rows, None, replicas, None), P()),
        out_specs=P(None, rows, None),
        check_vma=False,
    )
```

time: 112 us -> 108 us (0.964)
  starting transfers between devices: 16.5 us -> 10.8 us
  blocking collectives: 83 us -> 86 us
  Pallas kernels: 8.67 us -> 7.42 us
    ppermute x1, starting transfers between devices: 7.7 us -> 2.04 us  [on_device(): lax.ppermute(own, 'core', swap)]
    all_to_all x3 -> x4, blocking collectives: 51.5 us -> 55.5 us  [the longest x1 22.9 us: quarter_of(): return exchange(pieces, 'shard').reshape(order, width)]
    all_to_all x1, blocking collectives: 18.6 us -> 17.3 us  [on_device(): back = exchange(update.reshape(nz, ny, rows, width), 'shard')]
    pallas_call x4 -> x5, Pallas kernels: 6.68 us -> 5.91 us  [the longest x1 4.02 us: step(): call(functools.partial(step_kernel, first), shaped((order, width)), 'vvv'...]
where the time goes in v4:
time: 108 us
  blocking collectives  86 us (80%)
  starting transfers between devices  10.8 us (10%)
  Pallas kernels  7.42 us (7%)
  waiting for transfers between devices  3.58 us (3%)
    all_to_all x1, blocking collectives, quarter_of(): return exchange(pieces, 'shard').reshape(order, width)  22.9 us
    all_to_all x1, blocking collectives, on_device(): back = exchange(update.reshape(nz, ny, rows, width), 'shard')  17.3 us
    all_to_all x1, blocking collectives, on_device(): own = exchange(spread.reshape(nx * ny, nz, rows, width), ('x', 'tensor'))  13.3 us
    all_to_all x1, blocking collectives, stats_early(): exchange(call(fan_stats_kernel, shaped((nx, 4 * width, width)), 'v')(stat...  11.6 us
    all_to_all x1, blocking collectives, quarter_of(): exchange(pieces.reshape(nx * ny, nz, rows, width), ('x', 'tensor'))  11.6 us
    all_to_all x1, blocking collectives, stats_early(): return step(0, stat, exchange(quarters, 'x'), got_stat)  9.37 us
    ppermute x1, starting transfers between devices, on_device(): got = lax.ppermute(send, 'core', swap)  8.79 us
    pallas_call x1, Pallas kernels, step(): call(functools.partial(step_kernel, first), shaped((order, width)), 'vvv'...  4.02 us
  transfers between devices with their start and end apart: 2, of which 2 were waited for; matrix products, arithmetic and copies ran while one was open for 0% of the time, Pallas kernels for 0%

profile of v4, /device:TPU:1, one launch (start us, length us, event | category | flops | bytes accessed | tf_op | source)
XLA Modules:
  0.0 107.9 jit_solution(4256545014997955936)
XLA Ops:
  0.0 1.3 %shard_map.37 = (bf16[81,8,512]{2,1,0:T(8,128)(2,1)S(1)}, bf16[81,8,512]{2,1,0:T(8,128)(2,1)S(1)}) custom-call(s32[64]{0:T(128)} %slot_ref.1, bf16[1,64,8,512]{3,2,1,0:T(8,128)(2,1)} %grad_hbm.1, f32[2,2,64,512]{3,2,1,0:T(8,128)} %stat_hbm.1), custom_call_target="tpu_custom_call" | custom-call | bytes 1048576 | tf_op jit(solution)/shard_map/pallas_call | solution.py:257
  1.3 8.8 %collective-permute-start = (bf16[81,8,512]{2,1,0:T(8,128)(2,1)S(1)}, bf16[81,8,512]{2,1,0:T(8,128)(2,1)S(1)}, u32[]{:S(2)}, u32[]{:S(2)}) collective-permute-start(bf16[81,8,512]{2,1,0:T(8,128)(2,1)S(1)} %get-tuple-element.27), channel_id=1, source_target_pairs={{0,64},{64,0},{1,65},{65,1},{2,66},{66,2},{3,67},{67,3},{4,68},{68... | collective-permute-start | bytes 1990664 | tf_op jit(solution)/shard_map/ppermute | solution.py:268
  10.1 1.7 %collective-permute-done.got_ref = bf16[81,8,512]{2,1,0:T(8,128)(2,1)S(1)} collective-permute-done((bf16[81,8,512]{2,1,0:T(8,128)(2,1)S(1)}, bf16[81,8,512]{2,1,0:T(8,128)(2,1)S(1)}, u32[]{:S(2)}, u32[]{:S(2)}) %collective-permute-start) | collective-permute-done | bytes 663584 | tf_op jit(solution)/shard_map/ppermute | solution.py:268
  11.8 0.1 shard_map.38
  12.0 59.7 %conditional.1 = (bf16[512,128]{1,0:T(8,128)(2,1)S(1)}) conditional(s32[]{:T(128)} %convert_element_type.3, (bf16[2,128,512]{2,1,0:T(8,128)(2,1)S(1)}, bf16[4,4,16,8,128]{4,3,2,1,0:T(8,128)(2,1)S(1)}) %tuple.11, (bf16[4,4,16,8,128]{4,3,2,1,0:T(8,128)(2,1)S(1)}, bf16[2,128,512]{2,1,0:T(8,128)(2,1)S(1)}) %shard_map.38), branch_computations={%region_0.0_spmd, %region_1.0_spmd} | conditional | flops 2684354560 | bytes 8650760 | solution.py:310
  12.0 0.1 branch_0_fun.4
  12.1 11.6 %all_to_all.38.got_stat_ref = bf16[4,512,128]{2,1,0:T(8,128)(2,1)S(1)} all-to-all(bf16[4,512,128]{2,1,0:T(8,128)(2,1)S(1)} %branch_0_fun.4), channel_id=1, replica_groups=mesh['x'=4,'core'=2,'shard'=16,'tensor'=4] {'x'}, dimensions={0} | all-to-all | bytes 1048576 | tf_op jit(solution)/shard_map/cond/branch_0_fun/all_to_all | solution.py:305
  23.7 11.6 %all_to_all.39 = bf16[16,16,8,128]{3,2,1,0:T(8,128)(2,1)S(1)} all-to-all(bf16[16,16,8,128]{3,2,1,0:T(8,128)(2,1)S(1)} %bitcast.16), channel_id=1, replica_groups=mesh['x'=4,'core'=2,'shard'=16,'tensor'=4] {'x','tensor'}, dimensions={0} | all-to-all | bytes 1048576 | tf_op jit(solution)/shard_map/cond/branch_0_fun/all_to_all | solution.py:276
  35.2 0.1 branch_0_fun.5
  35.3 22.9 %all_to_all.40 = bf16[16,4,8,128]{3,2,1,0:T(8,128)(2,1)S(1)} all-to-all(bf16[16,4,8,128]{3,2,1,0:T(8,128)(2,1)S(1)} %branch_0_fun.5), channel_id=1, replica_groups=mesh['x'=4,'core'=2,'shard'=16,'tensor'=4] {'shard'}, dimensions={0} | all-to-all | bytes 262144 | tf_op jit(solution)/shard_map/cond/branch_0_fun/all_to_all | solution.py:278
  58.2 0.1 branch_0_fun.6
  58.3 9.4 %all_to_all.41.got_ref = bf16[4,512,128]{2,1,0:T(8,128)(2,1)S(1)} all-to-all(bf16[4,512,128]{2,1,0:T(8,128)(2,1)S(1)} %branch_0_fun.6), channel_id=1, replica_groups=mesh['x'=4,'core'=2,'shard'=16,'tensor'=4] {'x'}, dimensions={0} | all-to-all | bytes 1048576 | tf_op jit(solution)/shard_map/cond/branch_0_fun/all_to_all | solution.py:308
  67.7 4.0 %branch_0_fun.7 = bf16[512,128]{1,0:T(8,128)(2,1)S(1)} custom-call(bf16[2,128,512]{2,1,0:T(8,128)(2,1)S(1)} %get-tuple-element.16.stat_ref.own_ref, bf16[4,512,128]{2,1,0:T(8,128)(2,1)S(1)} %all_to_all.41.got_ref, bf16[4,512,128]{2,1,0:T(8,128)(2,1)S(1)} %all_to_all.38.got_stat_ref), custom_call_target="tpu_custom_call" | custom-call | flops 2684354560 | bytes 2097152 | tf_op jit(solution)/shard_map/cond/branch_0_fun/pallas_call | solution.py:281
  71.7 17.3 %all_to_all.45.in_ref = bf16[16,4,8,128]{3,2,1,0:T(8,128)(2,1)S(1)} all-to-all(bf16[16,4,8,128]{3,2,1,0:T(8,128)(2,1)S(1)} %bitcast.18), channel_id=1, replica_groups=mesh['x'=4,'core'=2,'shard'=16,'tensor'=4] {'shard'}, dimensions={0} | all-to-all | bytes 262144 | tf_op jit(solution)/shard_map/all_to_all | solution.py:311
  89.0 0.1 shard_map.39
  89.0 13.3 %all_to_all.46 = bf16[16,16,8,128]{3,2,1,0:T(8,128)(2,1)S(1)} all-to-all(bf16[16,16,8,128]{3,2,1,0:T(8,128)(2,1)S(1)} %bitcast.9), channel_id=1, replica_groups=mesh['x'=4,'core'=2,'shard'=16,'tensor'=4] {'x','tensor'}, dimensions={0} | all-to-all | bytes 1048576 | tf_op jit(solution)/shard_map/all_to_all | solution.py:313
  102.3 0.0 copy-start
  102.3 2.0 %collective-permute-start.1 = (bf16[4,4,16,8,128]{4,3,2,1,0:T(8,128)(2,1)S(1)}, bf16[4,4,16,8,128]{4,3,2,1,0:T(8,128)(2,1)S(1)}, u32[]{:S(2)}, u32[]{:S(2)}) collective-permute-start(bf16[4,4,16,8,128]{4,3,2,1,0:T(8,128)(2,1)S(1)} %bitcast.12), channel_id=1, source_target_pairs={{0,64},{64,0},{1,65},{65,1},{2,66},{66,2},{3,67},{67,3},{4,68},{68... | collective-permute-start | bytes 1572872 | tf_op jit(solution)/shard_map/ppermute | solution.py:325
  104.4 1.9 %collective-permute-done.1.got_ref = bf16[4,4,16,8,128]{4,3,2,1,0:T(8,128)(2,1)S(1)} collective-permute-done((bf16[4,4,16,8,128]{4,3,2,1,0:T(8,128)(2,1)S(1)}, bf16[4,4,16,8,128]{4,3,2,1,0:T(8,128)(2,1)S(1)}, u32[]{:S(2)}, u32[]{:S(2)}) %collective-permute-start.1) | collective-permute-done | bytes 524320 | tf_op jit(solution)/shard_map/ppermute | solution.py:325
  106.2 0.0 copy-done
  106.2 1.7 %shard_map.40 = bf16[64,8,512]{2,1,0:T(8,128)(2,1)} custom-call(s32[64]{0:T(128)S(1)} %copy-done, bf16[4,4,16,8,128]{4,3,2,1,0:T(8,128)(2,1)S(1)} %bitcast.13, bf16[4,4,16,8,128]{4,3,2,1,0:T(8,128)(2,1)S(1)} %collective-permute-done.1.got_ref), custom_call_target="tpu_custom_call" | custom-call | bytes 1048576 | tf_op jit(solution)/shard_map/pallas_call | solution.py:315
Async XLA Ops:
  1.3 10.5 %collective-permute-start = (bf16[81,8,512]{2,1,0:T(8,128)(2,1)S(1)}, bf16[81,8,512]{2,1,0:T(8,128)(2,1)S(1)}, u32[]{:S(2)}, u32[]{:S(2)}) collective-permute-start(bf16[81,8,512]{2,1,0:T(8,128)(2,1)S(1)} %get-tuple-element.27), channel_id=1, source_target_pairs={{0,64},{64,0},{1,65},{65,1},{2,66},{66,2},{3,67},{67,3},{4,68},{68... | collective-permute-start | bytes 1990664 | tf_op jit(solution)/shard_map/ppermute | solution.py:268
  102.3 3.9 %copy-start = (s32[64]{0:T(128)S(1)}, s32[64]{0:T(128)}, u32[]{:S(2)}) copy-start(s32[64]{0:T(128)} %slot_ref.1) | copy-start | bytes 772
  102.3 3.9 %collective-permute-start.1 = (bf16[4,4,16,8,128]{4,3,2,1,0:T(8,128)(2,1)S(1)}, bf16[4,4,16,8,128]{4,3,2,1,0:T(8,128)(2,1)S(1)}, u32[]{:S(2)}, u32[]{:S(2)}) collective-permute-start(bf16[4,4,16,8,128]{4,3,2,1,0:T(8,128)(2,1)S(1)} %bitcast.12), channel_id=1, source_target_pairs={{0,64},{64,0},{1,65},{65,1},{2,66},{66,2},{3,67},{67,3},{4,68},{68... | collective-permute-start | bytes 1572872 | tf_op jit(solution)/shard_map/ppermute | solution.py:325

commit v5 on v4

--- a/solution.py
+++ b/solution.py
@@ -207,6 +207,13 @@
     out_ref[...] = (pre_ref[:, at(0)] * scale).astype(BF)
 
 
+def fan_swap_kernel(in_ref, out_ref):
+    for part in range(in_ref.shape[1]):
+        piece = in_ref[:, part]
+        for chip in range(out_ref.shape[0]):
+            out_ref[chip, part] = piece
+
+
 def spread_kernel(in_ref, out_ref):
     nx, ny = out_ref.shape[:2]
     for part in range(ny):
@@ -232,10 +239,15 @@
             )
         return carry
 
-    lax.fori_loop(0, out.shape[0], move, 0, unroll=8)
-    store = pltpu.make_async_copy(out, out_hbm, sems.at[1])
-    store.start()
-    store.wait()
+    size = out.shape[0] // 2
+    stores = []
+    for half in range(2):
+        lax.fori_loop(half * size, (half + 1) * size, move, 0, unroll=8)
+        span = pl.ds(half * size, size)
+        stores.append(pltpu.make_async_copy(out.at[span], out_hbm.at[span], sems.at[1 + half]))
+        stores[-1].start()
+    for store in stores:
+        store.wait()
 
 
 def shaped(shape, dtype=BF):
@@ -296,22 +308,26 @@
             nbytes=2 << 20,
         )(*arrays)
 
+    def spread(update):
+        back = exchange(update.reshape(nz, ny, rows, width), "shard")
+        pieces = call(spread_kernel, shaped((nx, ny, nz, rows, width)), "v")(back)
+        return exchange(pieces.reshape(nx * ny, nz, rows, width), ("x", "tensor")).reshape(pieces.shape)
+
     def stats_late(pieces, stat):
         whole_shape = shaped((nx, order + 4 * width, width))
         both = exchange(call(fan_both_kernel, whole_shape, "vv")(quarter_of(pieces), stat), "x")
-        return step(order, stat, both, both)
+        return spread(step(order, stat, both, both))
 
     def stats_early(pieces, stat):
         got_stat = exchange(call(fan_stats_kernel, shaped((nx, 4 * width, width)), "v")(stat), "x")
         pieces, got_stat = lax.optimization_barrier((pieces, got_stat))
         quarters = call(fan_grad_kernel, shaped((nx, order, width)), "v")(quarter_of(pieces))
-        return step(0, stat, exchange(quarters, "x"), got_stat)
-
-    update = lax.cond(lax.axis_index("core") == 0, stats_late, stats_early, parts, stat)
-    back = exchange(update.reshape(nz, ny, rows, width), "shard")
-    spread = call(spread_kernel, shaped((nx, ny, nz, rows, width)), "v")(back)
-    own = exchange(spread.reshape(nx * ny, nz, rows, width), ("x", "tensor"))
-    own = own.reshape(nx, ny, nz, rows, width)
+        update = step(0, stat, exchange(quarters, "x"), got_stat)
+        back = exchange(update.reshape(nz * ny, rows, width), ("shard", "tensor")).reshape(nz, ny, rows, width)
+        back = call(fan_swap_kernel, shaped((nx, ny, nz, rows, width)), "v")(back)
+        return exchange(back, "x")
+
+    own = lax.cond(lax.axis_index("core") == 0, stats_late, stats_early, parts, stat)
     return call(
         pick_kernel,
         shaped((blocks, rows, order)),
@@ -319,7 +335,7 @@
         scratch=[
             pltpu.SMEM(owner_slot.shape, jnp.int32),
             pltpu.VMEM((blocks, rows, order), BF),
-            pltpu.SemaphoreType.DMA((2,)),
+            pltpu.SemaphoreType.DMA((3,)),
         ],
         out_kind="h",
     )(owner_slot, own, lax.ppermute(own, "core", swap))

time: 108 us -> 107 us (level)
  no operation moved by 1% of the time
where the time goes in v5:
time: 107 us
  blocking collectives  85.1 us (80%)
  starting transfers between devices  10.8 us (10%)
  Pallas kernels  7.34 us (7%)
  waiting for transfers between devices  3.58 us (3%)
    all_to_all x1, blocking collectives, quarter_of(): return exchange(pieces, 'shard').reshape(order, width)  22.9 us
    all_to_all x1, blocking collectives, stats_early(): exchange(update.reshape(nz * ny, rows, width), ('shard', 'tensor'))  20.3 us
    all_to_all x1, blocking collectives, stats_early(): exchange(call(fan_stats_kernel, shaped((nx, 4 * width, width)), 'v')(stat...  11.6 us
    all_to_all x1, blocking collectives, quarter_of(): exchange(pieces.reshape(nx * ny, nz, rows, width), ('x', 'tensor'))  11.6 us
    all_to_all x1, blocking collectives, stats_early(): update = step(0, stat, exchange(quarters, 'x'), got_stat)  9.37 us
    all_to_all x1, blocking collectives, stats_early(): return exchange(back, 'x')  9.33 us
    ppermute x1, starting transfers between devices, on_device(): got = lax.ppermute(send, 'core', swap)  8.79 us
    pallas_call x1, Pallas kernels, step(): call(functools.partial(step_kernel, first), shaped((order, width)), 'vvv'...  4.02 us
  transfers between devices with their start and end apart: 2, of which 2 were waited for; matrix products, arithmetic and copies ran while one was open for 0% of the time, Pallas kernels for 0%

profile of v5, /device:TPU:1, one launch (start us, length us, event | category | flops | bytes accessed | tf_op | source)
XLA Modules:
  0.0 106.9 jit_solution(3660701752917342376)
XLA Ops:
  0.0 1.3 %shard_map.37 = (bf16[81,8,512]{2,1,0:T(8,128)(2,1)S(1)}, bf16[81,8,512]{2,1,0:T(8,128)(2,1)S(1)}) custom-call(s32[64]{0:T(128)} %slot_ref.1, bf16[1,64,8,512]{3,2,1,0:T(8,128)(2,1)} %grad_hbm.1, f32[2,2,64,512]{3,2,1,0:T(8,128)} %stat_hbm.1), custom_call_target="tpu_custom_call" | custom-call | bytes 1048576 | tf_op jit(solution)/shard_map/pallas_call | solution.py:269
  1.3 8.8 %collective-permute-start = (bf16[81,8,512]{2,1,0:T(8,128)(2,1)S(1)}, bf16[81,8,512]{2,1,0:T(8,128)(2,1)S(1)}, u32[]{:S(2)}, u32[]{:S(2)}) collective-permute-start(bf16[81,8,512]{2,1,0:T(8,128)(2,1)S(1)} %get-tuple-element.27), channel_id=1, source_target_pairs={{0,64},{64,0},{1,65},{65,1},{2,66},{66,2},{3,67},{67,3},{4,68},{68... | collective-permute-start | bytes 1990664 | tf_op jit(solution)/shard_map/ppermute | solution.py:280
  10.1 1.7 %collective-permute-done.got_ref = bf16[81,8,512]{2,1,0:T(8,128)(2,1)S(1)} collective-permute-done((bf16[81,8,512]{2,1,0:T(8,128)(2,1)S(1)}, bf16[81,8,512]{2,1,0:T(8,128)(2,1)S(1)}, u32[]{:S(2)}, u32[]{:S(2)}) %collective-permute-start) | collective-permute-done | bytes 663584 | tf_op jit(solution)/shard_map/ppermute | solution.py:280
  11.8 0.1 shard_map.38
  12.0 89.4 %conditional.1 = (bf16[4,4,16,8,128]{4,3,2,1,0:T(8,128)(2,1)S(1)}) conditional(s32[]{:T(128)} %convert_element_type.3, (bf16[2,128,512]{2,1,0:T(8,128)(2,1)S(1)}, bf16[4,4,16,8,128]{4,3,2,1,0:T(8,128)(2,1)S(1)}) %tuple.11, (bf16[4,4,16,8,128]{4,3,2,1,0:T(8,128)(2,1)S(1)}, bf16[2,128,512]{2,1,0:T(8,128)(2,1)S(1)}) %shard_map.38), branch_computations={%region_0.0_spmd, %region_1.0_spmd} | conditional | flops 2684354560 | bytes 11010056 | solution.py:330
  12.0 0.1 branch_0_fun.5
  12.1 11.6 %all_to_all.44.got_stat_ref = bf16[4,512,128]{2,1,0:T(8,128)(2,1)S(1)} all-to-all(bf16[4,512,128]{2,1,0:T(8,128)(2,1)S(1)} %branch_0_fun.5), channel_id=1, replica_groups=mesh['x'=4,'core'=2,'shard'=16,'tensor'=4] {'x'}, dimensions={0} | all-to-all | bytes 1048576 | tf_op jit(solution)/shard_map/cond/branch_0_fun/all_to_all | solution.py:322
  23.7 11.6 %all_to_all.45 = bf16[16,16,8,128]{3,2,1,0:T(8,128)(2,1)S(1)} all-to-all(bf16[16,16,8,128]{3,2,1,0:T(8,128)(2,1)S(1)} %bitcast.19), channel_id=1, replica_groups=mesh['x'=4,'core'=2,'shard'=16,'tensor'=4] {'x','tensor'}, dimensions={0} | all-to-all | bytes 1048576 | tf_op jit(solution)/shard_map/cond/branch_0_fun/all_to_all | solution.py:288
  35.2 0.1 branch_0_fun.6
  35.3 22.9 %all_to_all.46 = bf16[16,4,8,128]{3,2,1,0:T(8,128)(2,1)S(1)} all-to-all(bf16[16,4,8,128]{3,2,1,0:T(8,128)(2,1)S(1)} %branch_0_fun.6), channel_id=1, replica_groups=mesh['x'=4,'core'=2,'shard'=16,'tensor'=4] {'shard'}, dimensions={0} | all-to-all | bytes 262144 | tf_op jit(solution)/shard_map/cond/branch_0_fun/all_to_all | solution.py:290
  58.2 0.1 branch_0_fun.7
  58.3 9.4 %all_to_all.47.got_ref = bf16[4,512,128]{2,1,0:T(8,128)(2,1)S(1)} all-to-all(bf16[4,512,128]{2,1,0:T(8,128)(2,1)S(1)} %branch_0_fun.7), channel_id=1, replica_groups=mesh['x'=4,'core'=2,'shard'=16,'tensor'=4] {'x'}, dimensions={0} | all-to-all | bytes 1048576 | tf_op jit(solution)/shard_map/cond/branch_0_fun/all_to_all | solution.py:325
  67.7 4.0 %branch_0_fun.8 = bf16[512,128]{1,0:T(8,128)(2,1)S(1)} custom-call(bf16[2,128,512]{2,1,0:T(8,128)(2,1)S(1)} %get-tuple-element.16.stat_ref.own_ref, bf16[4,512,128]{2,1,0:T(8,128)(2,1)S(1)} %all_to_all.47.got_ref, bf16[4,512,128]{2,1,0:T(8,128)(2,1)S(1)} %all_to_all.44.got_stat_ref), custom_call_target="tpu_custom_call" | custom-call | flops 2684354560 | bytes 2097152 | tf_op jit(solution)/shard_map/cond/branch_0_fun/pallas_call | solution.py:293
  71.7 20.3 %all_to_all.48 = bf16[64,8,128]{2,1,0:T(8,128)(2,1)S(1)} all-to-all(bf16[64,8,128]{2,1,0:T(8,128)(2,1)S(1)} %bitcast.17), channel_id=1, replica_groups=mesh['x'=4,'core'=2,'shard'=16,'tensor'=4] {'shard','tensor'}, dimensions={0} | all-to-all | bytes 262144 | tf_op jit(solution)/shard_map/cond/branch_0_fun/all_to_all | solution.py:326
  92.0 0.1 branch_0_fun.9
  92.1 9.3 %all_to_all.49 = bf16[4,4,16,8,128]{4,3,2,1,0:T(8,128)(2,1)S(1)} all-to-all(bf16[4,4,16,8,128]{4,3,2,1,0:T(8,128)(2,1)S(1)} %branch_0_fun.9), channel_id=1, replica_groups=mesh['x'=4,'core'=2,'shard'=16,'tensor'=4] {'x'}, dimensions={0} | all-to-all | bytes 1048576 | tf_op jit(solution)/shard_map/cond/branch_0_fun/all_to_all | solution.py:328
  101.4 0.0 copy-start
  101.4 2.0 %collective-permute-start.1 = (bf16[4,4,16,8,128]{4,3,2,1,0:T(8,128)(2,1)S(1)}, bf16[4,4,16,8,128]{4,3,2,1,0:T(8,128)(2,1)S(1)}, u32[]{:S(2)}, u32[]{:S(2)}) collective-permute-start(bf16[4,4,16,8,128]{4,3,2,1,0:T(8,128)(2,1)S(1)} %get-tuple-element.30.own_ref), channel_id=1, source_target_pairs={{0,64},{64,0},{1,65},{65,1},{2,66},{66,2},{3,67},{67,3},{4,68},{68... | collective-permute-start | bytes 1572872 | tf_op jit(solution)/shard_map/ppermute | solution.py:341
  103.5 1.9 %collective-permute-done.1.got_ref = bf16[4,4,16,8,128]{4,3,2,1,0:T(8,128)(2,1)S(1)} collective-permute-done((bf16[4,4,16,8,128]{4,3,2,1,0:T(8,128)(2,1)S(1)}, bf16[4,4,16,8,128]{4,3,2,1,0:T(8,128)(2,1)S(1)}, u32[]{:S(2)}, u32[]{:S(2)}) %collective-permute-start.1) | collective-permute-done | bytes 524320 | tf_op jit(solution)/shard_map/ppermute | solution.py:341
  105.3 0.0 copy-done
  105.3 1.6 %shard_map.39 = bf16[64,8,512]{2,1,0:T(8,128)(2,1)} custom-call(s32[64]{0:T(128)S(1)} %copy-done, bf16[4,4,16,8,128]{4,3,2,1,0:T(8,128)(2,1)S(1)} %get-tuple-element.30.own_ref, bf16[4,4,16,8,128]{4,3,2,1,0:T(8,128)(2,1)S(1)} %collective-permute-done.1.got_ref), custom_call_target="tpu_custom_call" | custom-call | bytes 1048576 | tf_op jit(solution)/shard_map/pallas_call | solution.py:331
Async XLA Ops:
  1.3 10.5 %collective-permute-start = (bf16[81,8,512]{2,1,0:T(8,128)(2,1)S(1)}, bf16[81,8,512]{2,1,0:T(8,128)(2,1)S(1)}, u32[]{:S(2)}, u32[]{:S(2)}) collective-permute-start(bf16[81,8,512]{2,1,0:T(8,128)(2,1)S(1)} %get-tuple-element.27), channel_id=1, source_target_pairs={{0,64},{64,0},{1,65},{65,1},{2,66},{66,2},{3,67},{67,3},{4,68},{68... | collective-permute-start | bytes 1990664 | tf_op jit(solution)/shard_map/ppermute | solution.py:280
  101.4 3.9 %copy-start = (s32[64]{0:T(128)S(1)}, s32[64]{0:T(128)}, u32[]{:S(2)}) copy-start(s32[64]{0:T(128)} %slot_ref.1) | copy-start | bytes 772
  101.4 3.9 %collective-permute-start.1 = (bf16[4,4,16,8,128]{4,3,2,1,0:T(8,128)(2,1)S(1)}, bf16[4,4,16,8,128]{4,3,2,1,0:T(8,128)(2,1)S(1)}, u32[]{:S(2)}, u32[]{:S(2)}) collective-permute-start(bf16[4,4,16,8,128]{4,3,2,1,0:T(8,128)(2,1)S(1)} %get-tuple-element.30.own_ref), channel_id=1, source_target_pairs={{0,64},{64,0},{1,65},{65,1},{2,66},{66,2},{3,67},{67,3},{4,68},{68... | collective-permute-start | bytes 1572872 | tf_op jit(solution)/shard_map/ppermute | solution.py:341

commit v6 on v5

--- a/solution.py
+++ b/solution.py
@@ -113,8 +113,30 @@
             out_ref[chip, start + width : start + 2 * width] = columns(side, 1 if shift < nx - 1 else 2)
 
 
-def fan_stats_kernel(stat_ref, out_ref):
-    fan_stats(stat_ref, out_ref, 0)
+def triangle(width):
+    row_ids = lax.broadcasted_iota(jnp.int32, (width, width), 0)
+    col_ids = lax.broadcasted_iota(jnp.int32, (width, width), 1)
+    return row_ids > col_ids, row_ids == col_ids
+
+
+def fan_packed_kernel(stat_ref, out_ref):
+    nx, rows, width = out_ref.shape
+    x = lax.axis_index("x")
+    below, on = triangle(width)
+
+    def columns(side, shift):
+        return stat_ref[side, :, pl.ds(pl.multiple_of(lax.rem(x + shift, nx) * width, width), width)]
+
+    left, right = columns(0, 0).astype(F32), columns(1, 0).astype(F32)
+    mixed = jnp.where(below, right, left).astype(BF)
+    line = jnp.sum(jnp.where(on, right, 0.0), axis=0, keepdims=True)
+    line = jnp.broadcast_to(line, (rows - 3 * width, width)).astype(BF)
+    for shift in range(1, nx):
+        chip = lax.rem(x - shift + nx, nx)
+        for side in range(2):
+            out_ref[chip, side * width : (side + 1) * width] = columns(side, 1 if shift < nx - 1 else 2)
+        out_ref[chip, 2 * width : 3 * width] = mixed
+        out_ref[chip, 3 * width :] = line
 
 
 def fan_grad_kernel(in_ref, out_ref):
@@ -164,9 +186,21 @@
             stat_ref[side, at(shift), at(0)] = block.T
             source = lax.rem(x + shift, nx)
             partner = shift % (nx - 1) + 1
-            base = first + 2 * side * width
-            stat_ref[side, at(shift), at(shift)] = got_stat_ref[source, base : base + width]
-            block = got_stat_ref[source, base + width : base + 2 * width]
+            if first:
+                base = first + 2 * side * width
+                own_block = got_stat_ref[source, base : base + width]
+                block = got_stat_ref[source, base + width : base + 2 * width]
+            else:
+                below, on = triangle(width)
+                mixed = got_stat_ref[source, 2 * width : 3 * width].astype(F32)
+                line = got_stat_ref[source, 3 * width :].astype(F32)[:1]
+                turned = mixed.T
+                if side == 0:
+                    own_block = jnp.where(below, turned, mixed).astype(BF)
+                else:
+                    own_block = jnp.where(below, mixed, jnp.where(on, line, turned)).astype(BF)
+                block = got_stat_ref[source, side * width : (side + 1) * width]
+            stat_ref[side, at(shift), at(shift)] = own_block
             stat_ref[side, at(shift), at(partner)] = block
             stat_ref[side, at(partner), at(shift)] = block.T
 
@@ -319,7 +353,7 @@
         return spread(step(order, stat, both, both))
 
     def stats_early(pieces, stat):
-        got_stat = exchange(call(fan_stats_kernel, shaped((nx, 4 * width, width)), "v")(stat), "x")
+        got_stat = exchange(call(fan_packed_kernel, shaped((nx, 3 * width + 16, width)), "v")(stat), "x")
         pieces, got_stat = lax.optimization_barrier((pieces, got_stat))
         quarters = call(fan_grad_kernel, shaped((nx, order, width)), "v")(quarter_of(pieces))
         update = step(0, stat, exchange(quarters, "x"), got_stat)

time: 107 us -> 108 us (level)
    all_to_all x1, blocking collectives: 11.6 us -> 10.3 us  [stats_early(): exchange(call(fan_packed_kernel, shaped((nx, 3 * width + 16, width)), 'v'...]
where the time goes in v6:
time: 108 us; the launch traced here: 107 us
  blocking collectives  85.2 us (79%)
  starting transfers between devices  10.8 us (10%)
  Pallas kernels  7.47 us (7%)
  waiting for transfers between devices  3.58 us (3%)
    all_to_all x1, blocking collectives, quarter_of(): return exchange(pieces, 'shard').reshape(order, width)  23.2 us
    all_to_all x1, blocking collectives, stats_early(): exchange(update.reshape(nz * ny, rows, width), ('shard', 'tensor'))  20.4 us
    all_to_all x1, blocking collectives, quarter_of(): exchange(pieces.reshape(nx * ny, nz, rows, width), ('x', 'tensor'))  11.6 us
    all_to_all x1, blocking collectives, stats_early(): update = step(0, stat, exchange(quarters, 'x'), got_stat)  10.4 us
    all_to_all x1, blocking collectives, stats_early(): exchange(call(fan_packed_kernel, shaped((nx, 3 * width + 16, width)), 'v'...  10.3 us
    all_to_all x1, blocking collectives, stats_early(): return exchange(back, 'x')  9.33 us
    ppermute x1, starting transfers between devices, on_device(): got = lax.ppermute(send, 'core', swap)  8.79 us
    pallas_call x1, Pallas kernels, step(): call(functools.partial(step_kernel, first), shaped((order, width)), 'vvv'...  4.16 us
  transfers between devices with their start and end apart: 2, of which 2 were waited for; matrix products, arithmetic and copies ran while one was open for 0% of the time, Pallas kernels for 0%

profile of v6, /device:TPU:1, one launch (start us, length us, event | category | flops | bytes accessed | tf_op | source)
XLA Modules:
  0.0 107.2 jit_solution(3742126689916292656)
XLA Ops:
  0.0 1.3 %shard_map.37 = (bf16[81,8,512]{2,1,0:T(8,128)(2,1)S(1)}, bf16[81,8,512]{2,1,0:T(8,128)(2,1)S(1)}) custom-call(s32[64]{0:T(128)} %slot_ref.1, bf16[1,64,8,512]{3,2,1,0:T(8,128)(2,1)} %grad_hbm.1, f32[2,2,64,512]{3,2,1,0:T(8,128)} %stat_hbm.1), custom_call_target="tpu_custom_call" | custom-call | bytes 1048576 | tf_op jit(solution)/shard_map/pallas_call | solution.py:303
  1.3 8.8 %collective-permute-start = (bf16[81,8,512]{2,1,0:T(8,128)(2,1)S(1)}, bf16[81,8,512]{2,1,0:T(8,128)(2,1)S(1)}, u32[]{:S(2)}, u32[]{:S(2)}) collective-permute-start(bf16[81,8,512]{2,1,0:T(8,128)(2,1)S(1)} %get-tuple-element.27), channel_id=1, source_target_pairs={{0,64},{64,0},{1,65},{65,1},{2,66},{66,2},{3,67},{67,3},{4,68},{68... | collective-permute-start | bytes 1990664 | tf_op jit(solution)/shard_map/ppermute | solution.py:314
  10.1 1.7 %collective-permute-done.got_ref = bf16[81,8,512]{2,1,0:T(8,128)(2,1)S(1)} collective-permute-done((bf16[81,8,512]{2,1,0:T(8,128)(2,1)S(1)}, bf16[81,8,512]{2,1,0:T(8,128)(2,1)S(1)}, u32[]{:S(2)}, u32[]{:S(2)}) %collective-permute-start) | collective-permute-done | bytes 663584 | tf_op jit(solution)/shard_map/ppermute | solution.py:314
  11.8 0.1 shard_map.38
  12.0 89.7 %conditional.1 = (bf16[4,4,16,8,128]{4,3,2,1,0:T(8,128)(2,1)S(1)}) conditional(s32[]{:T(128)} %convert_element_type.3, (bf16[2,128,512]{2,1,0:T(8,128)(2,1)S(1)}, bf16[4,4,16,8,128]{4,3,2,1,0:T(8,128)(2,1)S(1)}) %tuple.11, (bf16[4,4,16,8,128]{4,3,2,1,0:T(8,128)(2,1)S(1)}, bf16[2,128,512]{2,1,0:T(8,128)(2,1)S(1)}) %shard_map.38), branch_computations={%region_0.0_spmd, %region_1.0_spmd} | conditional | flops 2684354560 | bytes 10780680 | solution.py:364
  12.0 0.1 branch_0_fun.5
  12.0 10.3 %all_to_all.44.got_stat_ref = bf16[4,400,128]{2,1,0:T(8,128)(2,1)S(1)} all-to-all(bf16[4,400,128]{2,1,0:T(8,128)(2,1)S(1)} %branch_0_fun.5), channel_id=1, replica_groups=mesh['x'=4,'core'=2,'shard'=16,'tensor'=4] {'x'}, dimensions={0} | all-to-all | bytes 819200 | tf_op jit(solution)/shard_map/cond/branch_0_fun/all_to_all | solution.py:356
  22.3 11.6 %all_to_all.45 = bf16[16,16,8,128]{3,2,1,0:T(8,128)(2,1)S(1)} all-to-all(bf16[16,16,8,128]{3,2,1,0:T(8,128)(2,1)S(1)} %bitcast.19), channel_id=1, replica_groups=mesh['x'=4,'core'=2,'shard'=16,'tensor'=4] {'x','tensor'}, dimensions={0} | all-to-all | bytes 1048576 | tf_op jit(solution)/shard_map/cond/branch_0_fun/all_to_all | solution.py:322
  33.9 0.1 branch_0_fun.6
  34.0 23.2 %all_to_all.46 = bf16[16,4,8,128]{3,2,1,0:T(8,128)(2,1)S(1)} all-to-all(bf16[16,4,8,128]{3,2,1,0:T(8,128)(2,1)S(1)} %branch_0_fun.6), channel_id=1, replica_groups=mesh['x'=4,'core'=2,'shard'=16,'tensor'=4] {'shard'}, dimensions={0} | all-to-all | bytes 262144 | tf_op jit(solution)/shard_map/cond/branch_0_fun/all_to_all | solution.py:324
  57.2 0.1 branch_0_fun.7
  57.3 10.4 %all_to_all.47.got_ref = bf16[4,512,128]{2,1,0:T(8,128)(2,1)S(1)} all-to-all(bf16[4,512,128]{2,1,0:T(8,128)(2,1)S(1)} %branch_0_fun.7), channel_id=1, replica_groups=mesh['x'=4,'core'=2,'shard'=16,'tensor'=4] {'x'}, dimensions={0} | all-to-all | bytes 1048576 | tf_op jit(solution)/shard_map/cond/branch_0_fun/all_to_all | solution.py:359
  67.7 4.2 %branch_0_fun.8 = bf16[512,128]{1,0:T(8,128)(2,1)S(1)} custom-call(bf16[2,128,512]{2,1,0:T(8,128)(2,1)S(1)} %get-tuple-element.16.stat_ref.own_ref, bf16[4,512,128]{2,1,0:T(8,128)(2,1)S(1)} %all_to_all.47.got_ref, bf16[4,400,128]{2,1,0:T(8,128)(2,1)S(1)} %all_to_all.44.got_stat_ref), custom_call_target="tpu_custom_call" | custom-call | flops 2684354560 | bytes 2097152 | tf_op jit(solution)/shard_map/cond/branch_0_fun/pallas_call | solution.py:327
  71.8 20.4 %all_to_all.48 = bf16[64,8,128]{2,1,0:T(8,128)(2,1)S(1)} all-to-all(bf16[64,8,128]{2,1,0:T(8,128)(2,1)S(1)} %bitcast.17), channel_id=1, replica_groups=mesh['x'=4,'core'=2,'shard'=16,'tensor'=4] {'shard','tensor'}, dimensions={0} | all-to-all | bytes 262144 | tf_op jit(solution)/shard_map/cond/branch_0_fun/all_to_all | solution.py:360
  92.2 0.1 branch_0_fun.9
  92.3 9.3 %all_to_all.49 = bf16[4,4,16,8,128]{4,3,2,1,0:T(8,128)(2,1)S(1)} all-to-all(bf16[4,4,16,8,128]{4,3,2,1,0:T(8,128)(2,1)S(1)} %branch_0_fun.9), channel_id=1, replica_groups=mesh['x'=4,'core'=2,'shard'=16,'tensor'=4] {'x'}, dimensions={0} | all-to-all | bytes 1048576 | tf_op jit(solution)/shard_map/cond/branch_0_fun/all_to_all | solution.py:362
  101.6 0.0 copy-start
  101.6 2.0 %collective-permute-start.1 = (bf16[4,4,16,8,128]{4,3,2,1,0:T(8,128)(2,1)S(1)}, bf16[4,4,16,8,128]{4,3,2,1,0:T(8,128)(2,1)S(1)}, u32[]{:S(2)}, u32[]{:S(2)}) collective-permute-start(bf16[4,4,16,8,128]{4,3,2,1,0:T(8,128)(2,1)S(1)} %get-tuple-element.30.own_ref), channel_id=1, source_target_pairs={{0,64},{64,0},{1,65},{65,1},{2,66},{66,2},{3,67},{67,3},{4,68},{68... | collective-permute-start | bytes 1572872 | tf_op jit(solution)/shard_map/ppermute | solution.py:375
  103.7 1.9 %collective-permute-done.1.got_ref = bf16[4,4,16,8,128]{4,3,2,1,0:T(8,128)(2,1)S(1)} collective-permute-done((bf16[4,4,16,8,128]{4,3,2,1,0:T(8,128)(2,1)S(1)}, bf16[4,4,16,8,128]{4,3,2,1,0:T(8,128)(2,1)S(1)}, u32[]{:S(2)}, u32[]{:S(2)}) %collective-permute-start.1) | collective-permute-done | bytes 524320 | tf_op jit(solution)/shard_map/ppermute | solution.py:375
  105.6 0.0 copy-done
  105.6 1.6 %shard_map.39 = bf16[64,8,512]{2,1,0:T(8,128)(2,1)} custom-call(s32[64]{0:T(128)S(1)} %copy-done, bf16[4,4,16,8,128]{4,3,2,1,0:T(8,128)(2,1)S(1)} %get-tuple-element.30.own_ref, bf16[4,4,16,8,128]{4,3,2,1,0:T(8,128)(2,1)S(1)} %collective-permute-done.1.got_ref), custom_call_target="tpu_custom_call" | custom-call | bytes 1048576 | tf_op jit(solution)/shard_map/pallas_call | solution.py:365
Async XLA Ops:
  1.3 10.5 %collective-permute-start = (bf16[81,8,512]{2,1,0:T(8,128)(2,1)S(1)}, bf16[81,8,512]{2,1,0:T(8,128)(2,1)S(1)}, u32[]{:S(2)}, u32[]{:S(2)}) collective-permute-start(bf16[81,8,512]{2,1,0:T(8,128)(2,1)S(1)} %get-tuple-element.27), channel_id=1, source_target_pairs={{0,64},{64,0},{1,65},{65,1},{2,66},{66,2},{3,67},{67,3},{4,68},{68... | collective-permute-start | bytes 1990664 | tf_op jit(solution)/shard_map/ppermute | solution.py:314
  101.6 3.9 %copy-start = (s32[64]{0:T(128)S(1)}, s32[64]{0:T(128)}, u32[]{:S(2)}) copy-start(s32[64]{0:T(128)} %slot_ref.1) | copy-start | bytes 772
  101.6 3.9 %collective-permute-start.1 = (bf16[4,4,16,8,128]{4,3,2,1,0:T(8,128)(2,1)S(1)}, bf16[4,4,16,8,128]{4,3,2,1,0:T(8,128)(2,1)S(1)}, u32[]{:S(2)}, u32[]{:S(2)}) collective-permute-start(bf16[4,4,16,8,128]{4,3,2,1,0:T(8,128)(2,1)S(1)} %get-tuple-element.30.own_ref), channel_id=1, source_target_pairs={{0,64},{64,0},{1,65},{65,1},{2,66},{66,2},{3,67},{67,3},{4,68},{68... | collective-permute-start | bytes 1572872 | tf_op jit(solution)/shard_map/ppermute | solution.py:375

commit v7 on v5

--- a/solution.py
+++ b/solution.py
@@ -98,23 +98,34 @@
         out_ref[:, part] = total.astype(BF)
 
 
-def fan_stats(stat_ref, out_ref, base):
-    nx, _, width = out_ref.shape
+def triangle(width):
+    row_ids = lax.broadcasted_iota(jnp.int32, (width, width), 0)
+    col_ids = lax.broadcasted_iota(jnp.int32, (width, width), 1)
+    return row_ids > col_ids, row_ids == col_ids
+
+
+def fan_packed(stat_ref, out_ref, base):
+    nx, rows, width = out_ref.shape
     x = lax.axis_index("x")
+    below, on = triangle(width)
 
     def columns(side, shift):
         return stat_ref[side, :, pl.ds(pl.multiple_of(lax.rem(x + shift, nx) * width, width), width)]
 
+    left, right = columns(0, 0).astype(F32), columns(1, 0).astype(F32)
+    mixed = jnp.where(below, right, left).astype(BF)
+    line = jnp.sum(jnp.where(on, right, 0.0), axis=0, keepdims=True)
+    line = jnp.broadcast_to(line, (rows - base - 3 * width, width)).astype(BF)
     for shift in range(1, nx):
         chip = lax.rem(x - shift + nx, nx)
         for side in range(2):
-            start = base + 2 * side * width
-            out_ref[chip, start : start + width] = columns(side, 0)
-            out_ref[chip, start + width : start + 2 * width] = columns(side, 1 if shift < nx - 1 else 2)
-
-
-def fan_stats_kernel(stat_ref, out_ref):
-    fan_stats(stat_ref, out_ref, 0)
+            out_ref[chip, base + side * width : base + (side + 1) * width] = columns(side, 1 if shift < nx - 1 else 2)
+        out_ref[chip, base + 2 * width : base + 3 * width] = mixed
+        out_ref[chip, base + 3 * width :] = line
+
+
+def fan_packed_kernel(stat_ref, out_ref):
+    fan_packed(stat_ref, out_ref, 0)
 
 
 def fan_grad_kernel(in_ref, out_ref):
@@ -126,7 +137,7 @@
     order = in_ref.shape[0]
     for chip in range(out_ref.shape[0]):
         out_ref[chip, :order] = in_ref[...]
-    fan_stats(stat_ref, out_ref, order)
+    fan_packed(stat_ref, out_ref, order)
 
 
 def dot(left, right, contract=((1,), (0,))):
@@ -164,9 +175,18 @@
             stat_ref[side, at(shift), at(0)] = block.T
             source = lax.rem(x + shift, nx)
             partner = shift % (nx - 1) + 1
-            base = first + 2 * side * width
-            stat_ref[side, at(shift), at(shift)] = got_stat_ref[source, base : base + width]
-            block = got_stat_ref[source, base + width : base + 2 * width]
+            below, on = triangle(width)
+            start = first + 2 * width
+            mixed = got_stat_ref[source, start : start + width].astype(F32)
+            line = got_stat_ref[source, start + width :].astype(F32)[:1]
+            turned = mixed.T
+            if side == 0:
+                own_block = jnp.where(below, turned, mixed).astype(BF)
+            else:
+                own_block = jnp.where(below, mixed, jnp.where(on, line, turned)).astype(BF)
+            start = first + side * width
+            block = got_stat_ref[source, start : start + width]
+            stat_ref[side, at(shift), at(shift)] = own_block
             stat_ref[side, at(shift), at(partner)] = block
             stat_ref[side, at(partner), at(shift)] = block.T
 
@@ -314,12 +334,12 @@
         return exchange(pieces.reshape(nx * ny, nz, rows, width), ("x", "tensor")).reshape(pieces.shape)
 
     def stats_late(pieces, stat):
-        whole_shape = shaped((nx, order + 4 * width, width))
+        whole_shape = shaped((nx, order + 3 * width + 16, width))
         both = exchange(call(fan_both_kernel, whole_shape, "vv")(quarter_of(pieces), stat), "x")
         return spread(step(order, stat, both, both))
 
     def stats_early(pieces, stat):
-        got_stat = exchange(call(fan_stats_kernel, shaped((nx, 4 * width, width)), "v")(stat), "x")
+        got_stat = exchange(call(fan_packed_kernel, shaped((nx, 3 * width + 16, width)), "v")(stat), "x")
         pieces, got_stat = lax.optimization_barrier((pieces, got_stat))
         quarters = call(fan_grad_kernel, shaped((nx, order, width)), "v")(quarter_of(pieces))
         update = step(0, stat, exchange(quarters, "x"), got_stat)

time: 107 us -> 107 us (level)
    all_to_all x1, blocking collectives: 11.6 us -> 10.3 us  [stats_early(): exchange(call(fan_packed_kernel, shaped((nx, 3 * width + 16, width)), 'v'...]
where the time goes in v7:
time: 107 us; the launch traced here: 106 us
  blocking collectives  84.4 us (79%)
  starting transfers between devices  10.8 us (10%)
  Pallas kernels  7.46 us (7%)
  waiting for transfers between devices  3.58 us (3%)
    all_to_all x1, blocking collectives, quarter_of(): return exchange(pieces, 'shard').reshape(order, width)  23.2 us
    all_to_all x1, blocking collectives, stats_early(): exchange(update.reshape(nz * ny, rows, width), ('shard', 'tensor'))  20.3 us
    all_to_all x1, blocking collectives, quarter_of(): exchange(pieces.reshape(nx * ny, nz, rows, width), ('x', 'tensor'))  11.6 us
    all_to_all x1, blocking collectives, stats_early(): exchange(call(fan_packed_kernel, shaped((nx, 3 * width + 16, width)), 'v'...  10.3 us
    all_to_all x1, blocking collectives, stats_early(): update = step(0, stat, exchange(quarters, 'x'), got_stat)  9.74 us
    all_to_all x1, blocking collectives, stats_early(): return exchange(back, 'x')  9.33 us
    ppermute x1, starting transfers between devices, on_device(): got = lax.ppermute(send, 'core', swap)  8.79 us
    pallas_call x1, Pallas kernels, step(): call(functools.partial(step_kernel, first), shaped((order, width)), 'vvv'...  4.15 us
  transfers between devices with their start and end apart: 2, of which 2 were waited for; matrix products, arithmetic and copies ran while one was open for 0% of the time, Pallas kernels for 0%

profile of v7, /device:TPU:1, one launch (start us, length us, event | category | flops | bytes accessed | tf_op | source)
XLA Modules:
  0.0 106.4 jit_solution(7437150350219727472)
XLA Ops:
  0.0 1.3 %shard_map.37 = (bf16[81,8,512]{2,1,0:T(8,128)(2,1)S(1)}, bf16[81,8,512]{2,1,0:T(8,128)(2,1)S(1)}) custom-call(s32[64]{0:T(128)} %slot_ref.1, bf16[1,64,8,512]{3,2,1,0:T(8,128)(2,1)} %grad_hbm.1, f32[2,2,64,512]{3,2,1,0:T(8,128)} %stat_hbm.1), custom_call_target="tpu_custom_call" | custom-call | bytes 1048576 | tf_op jit(solution)/shard_map/pallas_call | solution.py:289
  1.3 8.8 %collective-permute-start = (bf16[81,8,512]{2,1,0:T(8,128)(2,1)S(1)}, bf16[81,8,512]{2,1,0:T(8,128)(2,1)S(1)}, u32[]{:S(2)}, u32[]{:S(2)}) collective-permute-start(bf16[81,8,512]{2,1,0:T(8,128)(2,1)S(1)} %get-tuple-element.27), channel_id=1, source_target_pairs={{0,64},{64,0},{1,65},{65,1},{2,66},{66,2},{3,67},{67,3},{4,68},{68... | collective-permute-start | bytes 1990664 | tf_op jit(solution)/shard_map/ppermute | solution.py:300
  10.1 1.7 %collective-permute-done.got_ref = bf16[81,8,512]{2,1,0:T(8,128)(2,1)S(1)} collective-permute-done((bf16[81,8,512]{2,1,0:T(8,128)(2,1)S(1)}, bf16[81,8,512]{2,1,0:T(8,128)(2,1)S(1)}, u32[]{:S(2)}, u32[]{:S(2)}) %collective-permute-start) | collective-permute-done | bytes 663584 | tf_op jit(solution)/shard_map/ppermute | solution.py:300
  11.8 0.1 shard_map.38
  12.0 88.9 %conditional.1 = (bf16[4,4,16,8,128]{4,3,2,1,0:T(8,128)(2,1)S(1)}) conditional(s32[]{:T(128)} %convert_element_type.3, (bf16[2,128,512]{2,1,0:T(8,128)(2,1)S(1)}, bf16[4,4,16,8,128]{4,3,2,1,0:T(8,128)(2,1)S(1)}) %tuple.11, (bf16[4,4,16,8,128]{4,3,2,1,0:T(8,128)(2,1)S(1)}, bf16[2,128,512]{2,1,0:T(8,128)(2,1)S(1)}) %shard_map.38), branch_computations={%region_0.0_spmd, %region_1.0_spmd} | conditional | flops 2684354560 | bytes 10780680 | solution.py:350
  12.0 0.1 branch_0_fun.5
  12.0 10.3 %all_to_all.44.got_stat_ref = bf16[4,400,128]{2,1,0:T(8,128)(2,1)S(1)} all-to-all(bf16[4,400,128]{2,1,0:T(8,128)(2,1)S(1)} %branch_0_fun.5), channel_id=1, replica_groups=mesh['x'=4,'core'=2,'shard'=16,'tensor'=4] {'x'}, dimensions={0} | all-to-all | bytes 819200 | tf_op jit(solution)/shard_map/cond/branch_0_fun/all_to_all | solution.py:342
  22.3 11.6 %all_to_all.45 = bf16[16,16,8,128]{3,2,1,0:T(8,128)(2,1)S(1)} all-to-all(bf16[16,16,8,128]{3,2,1,0:T(8,128)(2,1)S(1)} %bitcast.19), channel_id=1, replica_groups=mesh['x'=4,'core'=2,'shard'=16,'tensor'=4] {'x','tensor'}, dimensions={0} | all-to-all | bytes 1048576 | tf_op jit(solution)/shard_map/cond/branch_0_fun/all_to_all | solution.py:308
  33.9 0.1 branch_0_fun.6
  34.0 23.2 %all_to_all.46 = bf16[16,4,8,128]{3,2,1,0:T(8,128)(2,1)S(1)} all-to-all(bf16[16,4,8,128]{3,2,1,0:T(8,128)(2,1)S(1)} %branch_0_fun.6), channel_id=1, replica_groups=mesh['x'=4,'core'=2,'shard'=16,'tensor'=4] {'shard'}, dimensions={0} | all-to-all | bytes 262144 | tf_op jit(solution)/shard_map/cond/branch_0_fun/all_to_all | solution.py:310
  57.2 0.1 branch_0_fun.7
  57.3 9.7 %all_to_all.47.got_ref = bf16[4,512,128]{2,1,0:T(8,128)(2,1)S(1)} all-to-all(bf16[4,512,128]{2,1,0:T(8,128)(2,1)S(1)} %branch_0_fun.7), channel_id=1, replica_groups=mesh['x'=4,'core'=2,'shard'=16,'tensor'=4] {'x'}, dimensions={0} | all-to-all | bytes 1048576 | tf_op jit(solution)/shard_map/cond/branch_0_fun/all_to_all | solution.py:345
  67.0 4.2 %branch_0_fun.8 = bf16[512,128]{1,0:T(8,128)(2,1)S(1)} custom-call(bf16[2,128,512]{2,1,0:T(8,128)(2,1)S(1)} %get-tuple-element.16.stat_ref.own_ref, bf16[4,512,128]{2,1,0:T(8,128)(2,1)S(1)} %all_to_all.47.got_ref, bf16[4,400,128]{2,1,0:T(8,128)(2,1)S(1)} %all_to_all.44.got_stat_ref), custom_call_target="tpu_custom_call" | custom-call | flops 2684354560 | bytes 2097152 | tf_op jit(solution)/shard_map/cond/branch_0_fun/pallas_call | solution.py:313
  71.2 20.3 %all_to_all.48 = bf16[64,8,128]{2,1,0:T(8,128)(2,1)S(1)} all-to-all(bf16[64,8,128]{2,1,0:T(8,128)(2,1)S(1)} %bitcast.17), channel_id=1, replica_groups=mesh['x'=4,'core'=2,'shard'=16,'tensor'=4] {'shard','tensor'}, dimensions={0} | all-to-all | bytes 262144 | tf_op jit(solution)/shard_map/cond/branch_0_fun/all_to_all | solution.py:346
  91.4 0.1 branch_0_fun.9
  91.5 9.3 %all_to_all.49 = bf16[4,4,16,8,128]{4,3,2,1,0:T(8,128)(2,1)S(1)} all-to-all(bf16[4,4,16,8,128]{4,3,2,1,0:T(8,128)(2,1)S(1)} %branch_0_fun.9), channel_id=1, replica_groups=mesh['x'=4,'core'=2,'shard'=16,'tensor'=4] {'x'}, dimensions={0} | all-to-all | bytes 1048576 | tf_op jit(solution)/shard_map/cond/branch_0_fun/all_to_all | solution.py:348
  100.9 0.0 copy-start
  100.9 2.0 %collective-permute-start.1 = (bf16[4,4,16,8,128]{4,3,2,1,0:T(8,128)(2,1)S(1)}, bf16[4,4,16,8,128]{4,3,2,1,0:T(8,128)(2,1)S(1)}, u32[]{:S(2)}, u32[]{:S(2)}) collective-permute-start(bf16[4,4,16,8,128]{4,3,2,1,0:T(8,128)(2,1)S(1)} %get-tuple-element.30.own_ref), channel_id=1, source_target_pairs={{0,64},{64,0},{1,65},{65,1},{2,66},{66,2},{3,67},{67,3},{4,68},{68... | collective-permute-start | bytes 1572872 | tf_op jit(solution)/shard_map/ppermute | solution.py:361
  102.9 1.9 %collective-permute-done.1.got_ref = bf16[4,4,16,8,128]{4,3,2,1,0:T(8,128)(2,1)S(1)} collective-permute-done((bf16[4,4,16,8,128]{4,3,2,1,0:T(8,128)(2,1)S(1)}, bf16[4,4,16,8,128]{4,3,2,1,0:T(8,128)(2,1)S(1)}, u32[]{:S(2)}, u32[]{:S(2)}) %collective-permute-start.1) | collective-permute-done | bytes 524320 | tf_op jit(solution)/shard_map/ppermute | solution.py:361
  104.8 0.0 copy-done
  104.8 1.6 %shard_map.39 = bf16[64,8,512]{2,1,0:T(8,128)(2,1)} custom-call(s32[64]{0:T(128)S(1)} %copy-done, bf16[4,4,16,8,128]{4,3,2,1,0:T(8,128)(2,1)S(1)} %get-tuple-element.30.own_ref, bf16[4,4,16,8,128]{4,3,2,1,0:T(8,128)(2,1)S(1)} %collective-permute-done.1.got_ref), custom_call_target="tpu_custom_call" | custom-call | bytes 1048576 | tf_op jit(solution)/shard_map/pallas_call | solution.py:351
Async XLA Ops:
  1.3 10.5 %collective-permute-start = (bf16[81,8,512]{2,1,0:T(8,128)(2,1)S(1)}, bf16[81,8,512]{2,1,0:T(8,128)(2,1)S(1)}, u32[]{:S(2)}, u32[]{:S(2)}) collective-permute-start(bf16[81,8,512]{2,1,0:T(8,128)(2,1)S(1)} %get-tuple-element.27), channel_id=1, source_target_pairs={{0,64},{64,0},{1,65},{65,1},{2,66},{66,2},{3,67},{67,3},{4,68},{68... | collective-permute-start | bytes 1990664 | tf_op jit(solution)/shard_map/ppermute | solution.py:300
  100.9 3.9 %copy-start = (s32[64]{0:T(128)S(1)}, s32[64]{0:T(128)}, u32[]{:S(2)}) copy-start(s32[64]{0:T(128)} %slot_ref.1) | copy-start | bytes 772
  100.9 3.9 %collective-permute-start.1 = (bf16[4,4,16,8,128]{4,3,2,1,0:T(8,128)(2,1)S(1)}, bf16[4,4,16,8,128]{4,3,2,1,0:T(8,128)(2,1)S(1)}, u32[]{:S(2)}, u32[]{:S(2)}) collective-permute-start(bf16[4,4,16,8,128]{4,3,2,1,0:T(8,128)(2,1)S(1)} %get-tuple-element.30.own_ref), channel_id=1, source_target_pairs={{0,64},{64,0},{1,65},{65,1},{2,66},{66,2},{3,67},{67,3},{4,68},{68... | collective-permute-start | bytes 1572872 | tf_op jit(solution)/shard_map/ppermute | solution.py:361
